TPU v7x, 512 devices: a whole 4x8x8 slice. The times are simulated.
512 devices in a mesh: seq: 32 (over x, z), mp: 16 (over y, core).
Axes of the slice: x: 4, y: 8, z: 8, core: 2. Of those that a mesh axis runs over, the one named last changes fastest.
Arguments:
- inputs: bfloat16 [8192, 16384], P('seq', 'mp'), may hold values from -6 to 6
- conv_weight: float32 [4, 16384], P(None, 'mp'), may hold values from -3 to 3
- conv_bias: float32 [16384], P('mp'), may hold values from -3 to 3
- proj_weight: bfloat16 [16384, 544], P('mp'), may hold values from -0.046875 to 0.046875
- dt_weight: bfloat16 [512, 16384], P(None, 'mp'), may hold values from -0.25 to 0.25
- dt_bias: float32 [16384], P('mp'), may hold values from -6.9 to -2.3
- decay_rate: float32 [16384, 16], P('mp'), may hold values from 0.01 to 10
- skip_gain: float32 [16384], P('mp'), may hold values from 0.5 to 1.5
Outputs:
- scanned: bfloat16 [8192, 16384], P('seq', 'mp')
All inputs are finite; a program needn't handle non-finite values.
Results may differ from a plain program's by a relative error of at most 0.014.
Values may be sent and summed in bfloat16 or wider, within the bound.
No kernel may reach another device: no remote copies, remote signals or barrier semaphores. Data moves between devices by JAX's collectives and lax.ppermute only.
A program may use at most 64 MiB of HBM per device.

v0:
```python
import jax
import jax.numpy as jnp
from jax import lax
from jax.experimental import pallas as pl
from jax.experimental.pallas import tpu as pltpu
from jax.sharding import PartitionSpec as P

F32, BF16 = jnp.float32, jnp.bfloat16
STATE = 16
DT_RANK = 512
LANES, TILES = 128, 8
LOG2E = 1.4426950408889634
PACK = STATE * TILES + 2 * TILES
Z = 8
UNROLL = 8
VMEM = pl.BlockSpec(memory_space=pltpu.VMEM)


def params(mib):
    return pltpu.CompilerParams(vmem_limit_bytes=mib << 20)


def cost(flops):
    return pl.CostEstimate(flops=flops, bytes_accessed=flops // 4, transcendentals=flops // 8)


def taps(pad_ref, w_ref, b_ref, first, count):
    pre = b_ref[...] + w_ref[0:1, :] * pad_ref[first + 5 : first + 5 + count, :]
    for k in range(1, 4):
        pre = pre + w_ref[k : k + 1, :] * pad_ref[first + 5 + k : first + 5 + k + count, :]
    return pre / (1.0 + jnp.exp(-pre))


def mix_kernel(
    x_hbm, w_hbm, b_hbm, pw_hbm, dtw_hbm, dtb_hbm, decay_hbm, gain_hbm,
    mixed_ref, head_ref, w_ref, b_ref, pw_ref, dtw_ref, dtb_ref, rate_ref, gain_ref,
    x_ref, pad_ref, decay_ref, row_ref, sems,
):
    rows = x_hbm.shape[0]
    step, parts = 16, 4
    some = rows // parts
    small = [
        pltpu.make_async_copy(source, target, sems.at[i])
        for i, (source, target) in enumerate(((w_hbm, w_ref), (b_hbm, b_ref)))
    ]
    chunks = [
        pltpu.make_async_copy(x_hbm.at[pl.ds(some * i, some)], x_ref.at[pl.ds(some * i, some)], sems.at[2 + i])
        for i in range(parts)
    ]
    later = [
        pltpu.make_async_copy(source, target, sems.at[2 + parts + i])
        for i, (source, target) in enumerate(
            ((decay_hbm, decay_ref), (gain_hbm, row_ref), (pw_hbm, pw_ref), (dtw_hbm, dtw_ref), (dtb_hbm, dtb_ref))
        )
    ]
    for copy in small + chunks + later:
        copy.start()
    pad_ref[0:8, :] = jnp.zeros_like(pad_ref[0:8, :])
    for copy in small:
        copy.wait()
    for i, copy in enumerate(chunks):
        copy.wait()
        for r in range(some * i, some * (i + 1), step):
            pad_ref[8 + r : 8 + r + step, :] = x_ref[r : r + step, :].astype(F32)
            mixed_ref[r : r + step, :] = taps(pad_ref, w_ref, b_ref, r, step).astype(BF16)
    head_ref[...] = pad_ref[8:16, :]
    for copy in later:
        copy.wait()
    for j in range(TILES):
        c = slice(LANES * j, LANES * (j + 1))
        rate_ref[pl.ds(j, STATE, TILES), :] = decay_ref[:, c] * -LOG2E
        gain_ref[j : j + 1, :] = row_ref[:, c]


def mix(x, weight, bias, weight_t, dtw, dtb, decay, gain):
    rows, width = x.shape
    return pl.pallas_call(
        mix_kernel,
        out_shape=(
            pltpu.VMEM((rows, width), BF16),
            pltpu.VMEM((8, width), F32),
            pltpu.VMEM(weight.shape, F32),
            pltpu.VMEM(bias.shape, F32),
            pltpu.VMEM(weight_t.shape, BF16),
            pltpu.VMEM(dtw.shape, BF16),
            pltpu.VMEM(dtb.shape, F32),
            pltpu.VMEM((STATE * TILES, LANES), F32),
            pltpu.VMEM((TILES, LANES), F32),
        ),
        in_specs=[pl.BlockSpec(memory_space=pltpu.HBM)] * 8,
        out_specs=(VMEM,) * 9,
        scratch_shapes=[
            pltpu.VMEM((rows, width), BF16),
            pltpu.VMEM((rows + 8, width), F32),
            pltpu.VMEM(decay.shape, F32),
            pltpu.VMEM(gain.shape, F32),
            pltpu.SemaphoreType.DMA((11,)),
        ],
        compiler_params=params(60),
        cost_estimate=cost(20_000_000),
        name="mix",
    )(x, weight, bias, weight_t, dtw, dtb, decay, gain)


def project_kernel(first_ref, head_ref, halo_ref, w_ref, b_ref, pw_ref, mixed_ref, part_ref, pad_ref):
    pad_ref[0:8, :] = halo_ref[...].astype(F32)
    pad_ref[8:16, :] = head_ref[...]
    top = taps(pad_ref, w_ref, b_ref, 0, 8)
    mixed_ref[16:, :] = first_ref[16:, :]
    mixed_ref[0:16, :] = jnp.concatenate([top, first_ref[0:16, :].astype(F32)[8:16]], axis=0).astype(BF16)
    share = lax.dot_general(
        mixed_ref[...], pw_ref[...], (((1,), (1,)), ((), ())), preferred_element_type=F32
    ).astype(BF16)
    pairs = share.shape[0] // 32
    for to in range(2 * pairs):
        at = 16 * ((to % 2) * pairs + to // 2)
        part_ref[16 * to : 16 * (to + 1), :] = share[at : at + 16, :]


def project(first, head, halo, weight, bias, weight_t):
    rows, width = first.shape
    return pl.pallas_call(
        project_kernel,
        out_shape=(
            pltpu.VMEM((rows, width), BF16),
            jax.ShapeDtypeStruct((rows, weight_t.shape[0]), BF16),
        ),
        in_specs=[VMEM] * 6,
        out_specs=(VMEM,) * 2,
        scratch_shapes=[pltpu.VMEM((16, width), F32)],
        compiler_params=params(8),
        name="project",
    )(first, head, halo, weight, bias, weight_t)


def total_kernel(parts_ref, out_ref):
    rows = 16
    total = parts_ref[0:rows, :].astype(F32)
    for k in range(1, parts_ref.shape[0] // rows):
        total = total + parts_ref[rows * k : rows * (k + 1), :].astype(F32)
    for k in range(out_ref.shape[0] // rows):
        out_ref[rows * k : rows * (k + 1), :] = total.astype(BF16)


def total(parts):
    return pl.pallas_call(
        total_kernel,
        out_shape=jax.ShapeDtypeStruct((parts.shape[0] // 2, parts.shape[1]), BF16),
        in_specs=[VMEM],
        out_specs=VMEM,
        compiler_params=params(8),
        name="total",
    )(parts)


def spread(columns, first, count, out_ref):
    for n in range(count):
        out_ref[n] = jnp.broadcast_to(
            columns[:, first + n : first + n + 1], (columns.shape[0], LANES)
        )


def tile(n):
    return slice(TILES * n, TILES * (n + 1))


def token(t):
    return pl.ds(pl.multiple_of(t * TILES, TILES), TILES)


def split_sum(value):
    high = value.astype(BF16).astype(F32)
    return jnp.concatenate([high, value - high], axis=0)


def sums_of(got_ref, k):
    both = got_ref[PACK * (k + 1) - 2 * TILES : PACK * (k + 1), :].astype(F32)
    return both[:TILES] + both[TILES:]


def states_of(got_ref, k, n):
    return got_ref[PACK * k + TILES * n : PACK * k + TILES * (n + 2), :].astype(F32)


def state_kernel(
    g_ref, dtw_ref, dtb_ref, mixed_ref, rate_ref, dt_hbm, send_ref, dt_ref, dx_ref, bc_ref, sem
):
    rows, width = mixed_ref.shape
    low = g_ref[:, 0:DT_RANK]
    for c in range(0, width, 256):
        pre = jnp.dot(low, dtw_ref[:, c : c + 256], preferred_element_type=F32)
        pre = pre + dtb_ref[:, c : c + 256]
        dt = jnp.maximum(pre, 0.0) + jnp.log1p(jnp.exp(-jnp.abs(pre)))
        dx = dt * mixed_ref[:, c : c + 256].astype(F32)
        for h in range(2):
            at = pl.ds(c // LANES + h, rows, TILES)
            dt_ref[at, :] = dt[:, LANES * h : LANES * (h + 1)]
            dx_ref[at, :] = dx[:, LANES * h : LANES * (h + 1)]
    keep = pltpu.make_async_copy(dt_ref, dt_hbm, sem)
    keep.start()
    spread(g_ref[:, DT_RANK : DT_RANK + 2 * STATE].astype(F32), 0, STATE, bc_ref)

    def group(i, carry):
        states, total = list(carry[:STATE]), carry[STATE]
        t0 = pl.multiple_of(i * UNROLL, UNROLL)
        for r in range(UNROLL):
            dt, dx = dt_ref[token(t0 + r), :], dx_ref[token(t0 + r), :]
            total = total + dt
            for n in range(STATE):
                enter = jnp.broadcast_to(bc_ref[n, pl.ds(t0 + r, 1), :], dt.shape)
                states[n] = jnp.exp2(dt * rate_ref[tile(n), :]) * states[n] + dx * enter
        return (*states, total)

    zero = jnp.zeros((TILES, LANES), F32)
    final = lax.fori_loop(0, rows // UNROLL, group, (zero,) * (STATE + 1))
    pack = [jnp.concatenate(final[n : n + 2], axis=0).astype(BF16) for n in range(0, STATE, 2)]
    pack.append(split_sum(final[STATE]).astype(BF16))
    for k in range(send_ref.shape[0] // PACK):
        for i, piece in enumerate(pack):
            at = PACK * k + 2 * TILES * i
            send_ref[at : at + 2 * TILES, :] = piece
    keep.wait()


def state(g, dtw, dtb, mixed, rate):
    rows, width = mixed.shape
    return pl.pallas_call(
        state_kernel,
        out_shape=(
            pltpu.HBM((rows * TILES, LANES), F32),
            jax.ShapeDtypeStruct((Z * PACK, LANES), BF16),
        ),
        in_specs=[VMEM] * 5,
        out_specs=(pl.BlockSpec(memory_space=pltpu.HBM), VMEM),
        scratch_shapes=[
            pltpu.VMEM((rows * TILES, LANES), F32),
            pltpu.VMEM((rows * TILES, LANES), F32),
            pltpu.VMEM((STATE, rows, LANES), F32),
            pltpu.SemaphoreType.DMA,
        ],
        compiler_params=params(12),
        name="state",
    )(g, dtw, dtb, mixed, rate)


def local_kernel(
    g_ref, dt_ref, rate_ref, mixed_ref, gain_ref, y_ref, cum_ref, rate_out, x_ref, bc_ref
):
    rows = mixed_ref.shape[0]
    rate_out[...] = rate_ref[...]
    spread(g_ref[:, DT_RANK : DT_RANK + 2 * STATE].astype(F32), 0, 2 * STATE, bc_ref)
    for j in range(TILES):
        x_ref[pl.ds(j, rows, TILES), :] = mixed_ref[:, LANES * j : LANES * (j + 1)].astype(F32)

    def group(i, carry):
        states, total = list(carry[:STATE]), carry[STATE]
        t0 = pl.multiple_of(i * UNROLL, UNROLL)
        for r in range(UNROLL):
            t = t0 + r
            dt, x = dt_ref[token(t), :], x_ref[token(t), :]
            dx, y = dt * x, gain_ref[...] * x
            total = total + dt
            cum_ref[token(t), :] = total
            for n in range(STATE):
                enter = jnp.broadcast_to(bc_ref[n, pl.ds(t, 1), :], dt.shape)
                read = jnp.broadcast_to(bc_ref[STATE + n, pl.ds(t, 1), :], dt.shape)
                states[n] = jnp.exp2(dt * rate_ref[tile(n), :]) * states[n] + dx * enter
                y = y + states[n] * read
            y_ref[token(t), :] = y
        return (*states, total)

    zero = jnp.zeros((TILES, LANES), F32)
    lax.fori_loop(0, rows // UNROLL, group, (zero,) * (STATE + 1))


def local(g, dt, rate, mixed, gain):
    rows = mixed.shape[0]
    flat = pltpu.VMEM((rows * TILES, LANES), F32)
    return pl.pallas_call(
        local_kernel,
        out_shape=(flat, flat, pltpu.VMEM(rate.shape, F32)),
        in_specs=[VMEM] * 5,
        out_specs=(VMEM,) * 3,
        scratch_shapes=[flat, pltpu.VMEM((2 * STATE, rows, LANES), F32)],
        compiler_params=params(12),
        cost_estimate=cost(60_000_000),
        name="local",
    )(g, dt, rate, mixed, gain)


def merge_kernel(place_ref, got_ref, rate_ref, send_ref, state_ref, sum_ref):
    rows, count = send_ref.shape[0] // PACK, got_ref.shape[0] // PACK
    z, x = place_ref[0], place_ref[1]
    zero = jnp.zeros((TILES, LANES), F32)
    sums = [sums_of(got_ref, k) for k in range(count)]
    whole, before = zero, zero
    for k in range(count):
        whole = whole + sums[k]
        before = before + jnp.where(k < z, sums[k], 0.0)
    sum_ref[...] = before
    for n in range(0, STATE, 2):
        blocks = [states_of(got_ref, k, n) for k in range(count)]
        ends, held = [], []
        for h in range(2):
            run, keep = zero, zero
            for k in range(count):
                keep = jnp.where(k == z, run, keep)
                run = jnp.exp2(sums[k] * rate_ref[tile(n + h), :]) * run + blocks[k][tile(h)]
            ends.append(run)
            held.append(keep)
        state_ref[TILES * n : TILES * (n + 2), :] = jnp.concatenate(held, axis=0)
        both = jnp.concatenate(ends, axis=0)
        for d in range(rows):
            at = PACK * d + TILES * n
            send_ref[at : at + 2 * TILES, :] = jnp.where(d > x, both, 0.0).astype(BF16)
    both = split_sum(whole)
    for d in range(rows):
        send_ref[PACK * (d + 1) - 2 * TILES : PACK * (d + 1), :] = jnp.where(d > x, both, 0.0).astype(BF16)


def merge(place, got, rate, rows):
    return pl.pallas_call(
        merge_kernel,
        out_shape=(
            jax.ShapeDtypeStruct((rows * PACK, LANES), BF16),
            pltpu.VMEM((STATE * TILES, LANES), F32),
            pltpu.VMEM((TILES, LANES), F32),
        ),
        in_specs=[pl.BlockSpec(memory_space=pltpu.SMEM), VMEM, VMEM],
        out_specs=(VMEM,) * 3,
        compiler_params=params(8),
        name="merge",
    )(place, got, rate)


def finish_kernel(got_ref, state_ref, sum_ref, rate_ref, g_ref, y_ref, cum_ref, out_ref, tot_ref, bc_ref):
    rows = out_ref.shape[0]
    spread(g_ref[:, DT_RANK : DT_RANK + 2 * STATE].astype(F32), STATE, STATE, bc_ref)
    count = got_ref.shape[0] // PACK - 1
    sums = [sums_of(got_ref, k) for k in range(count)]
    incoming = []
    for n in range(0, STATE, 2):
        blocks = [states_of(got_ref, k, n) for k in range(count)]
        for h in range(2):
            rate = rate_ref[tile(n + h), :]
            run = blocks[0][tile(h)]
            for k in range(1, count):
                run = jnp.exp2(sums[k] * rate) * run + blocks[k][tile(h)]
            incoming.append(jnp.exp2(sum_ref[...] * rate) * run + state_ref[tile(n + h), :])

    def group(i, carry):
        t0 = pl.multiple_of(i * UNROLL, UNROLL)
        for r in range(UNROLL):
            t = t0 + r
            cum, y = cum_ref[token(t), :], y_ref[token(t), :]
            for n in range(STATE):
                read = jnp.broadcast_to(bc_ref[n, pl.ds(t, 1), :], cum.shape)
                y = y + jnp.exp2(cum * rate_ref[tile(n), :]) * (carry[n] * read)
            tot_ref[token(t), :] = y
        return carry

    lax.fori_loop(0, rows // UNROLL, group, tuple(incoming))
    for j in range(TILES):
        out_ref[:, LANES * j : LANES * (j + 1)] = tot_ref[pl.ds(j, rows, TILES), :].astype(BF16)


def finish(got, states, sums, rate, g, y, cum):
    rows = g.shape[0]
    return pl.pallas_call(
        finish_kernel,
        out_shape=jax.ShapeDtypeStruct((rows, TILES * LANES), BF16),
        in_specs=[VMEM] * 7,
        out_specs=VMEM,
        scratch_shapes=[pltpu.VMEM(y.shape, F32), pltpu.VMEM((STATE, rows, LANES), F32)],
        compiler_params=params(8),
        name="finish",
    )(got, states, sums, rate, g, y, cum)


def shards(inputs, conv_weight, conv_bias, proj_weight, dt_weight, dt_bias, decay_rate, skip_gain):
    rows, width = inputs.shape
    seq, mp = lax.axis_size("seq"), lax.axis_size("mp")
    x_size, y_size = seq // Z, mp // 2
    on_z = [[Z * x + z for z in range(Z)] for x in range(x_size)]
    on_x = [[Z * x + z for x in range(x_size)] for z in range(Z)]
    on_y = [[2 * y + core for y in range(y_size)] for core in range(2)]
    on_chip = [[2 * y, 2 * y + 1] for y in range(y_size)]
    me = lax.axis_index("seq")
    place = jnp.stack([me % Z, me // Z]).astype(jnp.int32)
    halo = lax.ppermute(inputs[rows - 8 :], "seq", [(s, s + 1) for s in range(seq - 1)])
    first, head, taps_in, bias, weight, dtw, dtb, rate, gain = mix(
        inputs,
        conv_weight,
        conv_bias.reshape(1, width),
        jnp.transpose(proj_weight),
        dt_weight,
        dt_bias.reshape(1, width),
        jnp.transpose(decay_rate),
        skip_gain.reshape(1, width),
    )
    mixed, part = project(first, head, halo, taps_in, bias, weight)
    parts = lax.all_to_all(part, "mp", 0, 0, tiled=True)
    mine = lax.all_to_all(total(parts), "mp", 0, 0, tiled=True, axis_index_groups=on_y)
    projected = lax.all_gather(mine, "mp", axis=0, tiled=True, axis_index_groups=on_chip)
    dt, ends = state(projected, dtw, dtb, mixed, rate)
    got = lax.all_to_all(ends, "seq", 0, 0, tiled=True, axis_index_groups=on_z)
    y, cum, rate = local(projected, dt, rate, mixed, gain)
    ends, states, sums = merge(place, got, rate, x_size)
    got = lax.all_to_all(ends, "seq", 0, 0, tiled=True, axis_index_groups=on_x)
    return finish(got, states, sums, rate, projected, y, cum)


def solution(mesh):
    placed = (
        P("seq", "mp"),
        P(None, "mp"),
        P("mp"),
        P("mp", None),
        P(None, "mp"),
        P("mp"),
        P("mp", None),
        P("mp"),
    )
    return jax.shard_map(
        shards, mesh=mesh, in_specs=placed, out_specs=P("seq", "mp"), check_vma=False
    )
```

profile of v0, /device:TPU:2, one launch (start us, length us, event | category | flops | bytes accessed | tf_op | source)
XLA Modules:
  0.0 86.0 jit_solution(6294457016145284940)
XLA Ops:
  0.0 0.7 slice.3
  0.7 4.3 %collective-permute-start = (bf16[8,1024]{1,0:T(8,128)(2,1)S(1)}, bf16[8,1024]{1,0:T(8,128)(2,1)S(1)}, u32[]{:S(2)}, u32[]{:S(2)}) collective-permute-start(bf16[8,1024]{1,0:T(8,128)(2,1)S(1)} %slice.3), channel_id=1, source_target_pairs={{0,16},{16,32},{32,48},{48,64},{64,80},{80,96},{96,112},{112,128},... | collective-permute-start | bytes 49160 | tf_op jit(solution)/shard_map/ppermute | solution.py:390
  5.0 2.3 %mix.1 = (bf16[256,1024]{1,0:T(8,128)(2,1)S(1)}, f32[8,1024]{1,0:T(8,128)S(1)}, f32[4,1024]{1,0:T(4,128)S(1)}, f32[1,1024]{1,0:T(1,128)S(1)}, bf16[544,1024]{1,0...) custom-call(bf16[256,1024]{1,0:T(8,128)(2,1)} %x_hbm.1, ...), custom_call_target="tpu_custom_call" | custom-call | flops 20000000 | bytes 5000000 | tf_op jit(solution)/shard_map/mix/pallas_call | solution.py:77
  7.3 6.0 %collective-permute-done.halo_ref = bf16[8,1024]{1,0:T(8,128)(2,1)S(1)} collective-permute-done((bf16[8,1024]{1,0:T(8,128)(2,1)S(1)}, bf16[8,1024]{1,0:T(8,128)(2,1)S(1)}, u32[]{:S(2)}, u32[]{:S(2)}) %collective-permute-start) | collective-permute-done | bytes 16416 | tf_op jit(solution)/shard_map/ppermute | solution.py:390
  13.3 0.6 project.1
  14.0 19.4 %all_to_all.45 = bf16[16,16,544]{2,1,0:T(8,128)(2,1)S(1)} all-to-all(bf16[16,16,544]{2,1,0:T(8,128)(2,1)S(1)} %bitcast.19), channel_id=1, replica_groups=mesh['seq'=32,'mp'=16] {'mp'}, dimensions={0} | all-to-all | bytes 557056 | tf_op jit(solution)/shard_map/all_to_all | solution.py:402
  33.4 0.1 total.1
  33.4 13.7 %all_to_all.46 = bf16[8,16,544]{2,1,0:T(8,128)(2,1)S(1)} all-to-all(bf16[8,16,544]{2,1,0:T(8,128)(2,1)S(1)} %bitcast.17), channel_id=1, replica_groups={{0,2,4,6,8,10,12,14},{1,3,5,7,9,11,13,15},{16,18,20,22,24,26,28,30},{17..., dimensions={0} | all-to-all | bytes 278528 | tf_op jit(solution)/shard_map/all_to_all | solution.py:403
  47.1 2.0 %all_gather.3.g_ref = bf16[256,544]{1,0:T(8,128)(2,1)S(1)} all-gather(bf16[128,544]{1,0:T(8,128)(2,1)S(1)} %bitcast.21), channel_id=1, replica_groups={{0,1},{2,3},{4,5},{6,7},{8,9},{10,11},{12,13},{14,15},{16,17},{18,19},{..., dimensions={0}, use_global_device_ids=true | all-gather | bytes 417792 | tf_op jit(solution)/shard_map/all_gather | solution.py:404
  49.1 4.9 %state.1 = (f32[2048,128]{1,0:T(8,128)}, bf16[1152,128]{1,0:T(8,128)(2,1)}) custom-call(bf16[256,544]{1,0:T(8,128)(2,1)S(1)} %all_gather.3.g_ref, bf16[512,1024]{1,0:T(8,128)(2,1)S(1)} %get-tuple-element.30.dtw_ref, f32[1,1024]{1,0:T(1,128)S(1)} %get-tuple-element.31.dtb_ref, bf16[256,1024]{1,0:T(8,128)(2,1)S(1)} %get-tuple-element.32.mixed_ref, ...), custom_call_target="tpu_custom_call" | custom-call | tf_op jit(solution)/shard_map/state/pallas_call | solution.py:227
  54.0 4.5 %all-to-all-start.2 = ((bf16[8,144,128]{2,1,0:T(8,128)(2,1)}), bf16[8,144,128]{2,1,0:T(8,128)(2,1)S(1)}, u32[]{:S(2)}, u32[]{:S(2)}) async-start(bf16[8,144,128]{2,1,0:T(8,128)(2,1)} %bitcast.11), calls=%async_computation.2 | async-start | bytes 589824 | tf_op jit(solution)/shard_map/all_to_all | solution.py:406
  58.6 0.1 pad_add_fusion.place_ref
  58.6 0.0 copy-start
  58.6 1.2 %copy-done = f32[2048,128]{1,0:T(8,128)S(1)} copy-done((f32[2048,128]{1,0:T(8,128)S(1)}, f32[2048,128]{1,0:T(8,128)}, u32[]{:S(2)}) %copy-start) | copy-done | bytes 1048600
  59.9 5.3 %local.1 = (f32[2048,128]{1,0:T(8,128)S(1)}, f32[2048,128]{1,0:T(8,128)S(1)}, f32[128,128]{1,0:T(8,128)S(1)}) custom-call(bf16[256,544]{1,0:T(8,128)(2,1)S(1)} %all_gather.3.g_ref, f32[2048,128]{1,0:T(8,128)S(1)} %copy-done, f32[128,128]{1,0:T(8,128)S(1)} %get-tuple-element.33.rate_ref, bf16[256,1024]{1,0:T(8,128)(2,1)S(1)} %get-tuple-element.32.mixed_ref, ...), custom_call_target="tpu_custom_call" | custom-call | flops 60000000 | bytes 15000000 | tf_op jit(solution)/shard_map/local/pallas_call | solution.py:279
  65.2 6.3 %all-to-all-done.2 = bf16[8,144,128]{2,1,0:T(8,128)(2,1)S(1)} async-done(((bf16[8,144,128]{2,1,0:T(8,128)(2,1)}), bf16[8,144,128]{2,1,0:T(8,128)(2,1)S(1)}, u32[]{:S(2)}, u32[]{:S(2)}) %all-to-all-start.2) | async-done | bytes 294944 | tf_op jit(solution)/shard_map/all_to_all | solution.py:406
  71.4 0.7 merge.1
  72.1 9.2 %all_to_all.47 = bf16[4,144,128]{2,1,0:T(8,128)(2,1)S(1)} all-to-all(bf16[4,144,128]{2,1,0:T(8,128)(2,1)S(1)} %bitcast.20), channel_id=1, replica_groups={{0,128,256,384},{16,144,272,400},{32,160,288,416},{48,176,304,432},{64,..., dimensions={0} | all-to-all | bytes 294912 | tf_op jit(solution)/shard_map/all_to_all | solution.py:409
  81.4 4.6 %finish.1 = bf16[256,1024]{1,0:T(8,128)(2,1)} custom-call(bf16[576,128]{1,0:T(8,128)(2,1)S(1)} %bitcast.18, f32[128,128]{1,0:T(8,128)S(1)} %get-tuple-element.39.state_ref, f32[8,128]{1,0:T(8,128)S(1)} %get-tuple-element.40.sum_ref, f32[128,128]{1,0:T(8,128)S(1)} %get-tuple-element.37.rate_ref, bf16[256,544]{1,0:T(8,128)(2,1)S(1)} %all_gather.3.g_ref, ...), custom_call_target="tpu_custom_call" | custom-call | tf_op jit(solution)/shard_map/finish/pallas_call | solution.py:369
Async XLA Ops:
  0.7 12.6 %collective-permute-start = (bf16[8,1024]{1,0:T(8,128)(2,1)S(1)}, bf16[8,1024]{1,0:T(8,128)(2,1)S(1)}, u32[]{:S(2)}, u32[]{:S(2)}) collective-permute-start(bf16[8,1024]{1,0:T(8,128)(2,1)S(1)} %slice.3), channel_id=1, source_target_pairs={{0,16},{16,32},{32,48},{48,64},{64,80},{80,96},{96,112},{112,128},... | collective-permute-start | bytes 49160 | tf_op jit(solution)/shard_map/ppermute | solution.py:390
  54.0 17.4 %all-to-all-start.2 = ((bf16[8,144,128]{2,1,0:T(8,128)(2,1)}), bf16[8,144,128]{2,1,0:T(8,128)(2,1)S(1)}, u32[]{:S(2)}, u32[]{:S(2)}) async-start(bf16[8,144,128]{2,1,0:T(8,128)(2,1)} %bitcast.11), calls=%async_computation.2 | async-start | bytes 589824 | tf_op jit(solution)/shard_map/all_to_all | solution.py:406
  58.6 1.2 %copy-start = (f32[2048,128]{1,0:T(8,128)S(1)}, f32[2048,128]{1,0:T(8,128)}, u32[]{:S(2)}) copy-start(f32[2048,128]{1,0:T(8,128)} %get-tuple-element.35.dt_ref) | copy-start | bytes 3145732
where the time goes:
time: 86.4 us; the launch traced here: 86 us
  blocking collectives  44.4 us (51%)
  Pallas kernels  18.5 us (21%)
  waiting for transfers between devices  12.3 us (14%)
  starting transfers between devices  8.77 us (10%)
  local copies, waits for them, and re-layouts  1.94 us (2%)
    all_to_all x1, blocking collectives, shards(): parts = lax.all_to_all(part, 'mp', 0, 0, tiled=True)  19.4 us
    all_to_all x1, blocking collectives, shards(): lax.all_to_all(total(parts), 'mp', 0, 0, tiled=True, axis_index_groups=on_y)  13.7 us
    all_to_all x1, blocking collectives, shards(): got = lax.all_to_all(ends, 'seq', 0, 0, tiled=True, axis_index_groups=on_x)  9.24 us
    all_to_all x1, waiting for transfers between devices, shards(): got = lax.all_to_all(ends, 'seq', 0, 0, tiled=True, axis_index_groups=on_z)  6.28 us
    ppermute x1, waiting for transfers between devices, shards(): lax.ppermute(inputs[rows - 8:], 'seq', [(s, s + 1) for s in range(seq - 1)])  6.01 us
    pallas_call x1, Pallas kernels, local(): pl.pallas_call(local_kernel, out_shape=(flat, flat, pltpu.VMEM(rate.shape...  5.29 us
    pallas_call x1, Pallas kernels, state(): pl.pallas_call(state_kernel, out_shape=(pltpu.HBM((rows * TILES, LANES),...  4.9 us
    pallas_call x1, Pallas kernels, finish(): pl.pallas_call(finish_kernel, out_shape=jax.ShapeDtypeStruct((rows, TILES...  4.63 us
  transfers between devices with their start and end apart: 2, of which 2 were waited for; matrix products, arithmetic and copies ran while one was open for 0% of the time, Pallas kernels for 9%

commit v1 on v0

--- a/solution.py
+++ b/solution.py
@@ -12,8 +12,9 @@
 LOG2E = 1.4426950408889634
 PACK = STATE * TILES + 2 * TILES
 Z = 8
-UNROLL = 8
+UNROLL = 16
 VMEM = pl.BlockSpec(memory_space=pltpu.VMEM)
+SMEM = pl.BlockSpec(memory_space=pltpu.SMEM)
 
 
 def params(mib):
@@ -102,35 +103,56 @@
     )(x, weight, bias, weight_t, dtw, dtb, decay, gain)
 
 
-def project_kernel(first_ref, head_ref, halo_ref, w_ref, b_ref, pw_ref, mixed_ref, part_ref, pad_ref):
+def project_kernel(
+    place_ref, first_ref, head_ref, halo_ref, w_ref, b_ref, pw_ref, mixed_ref, share_ref, send_ref, pad_ref
+):
     pad_ref[0:8, :] = halo_ref[...].astype(F32)
     pad_ref[8:16, :] = head_ref[...]
     top = taps(pad_ref, w_ref, b_ref, 0, 8)
     mixed_ref[16:, :] = first_ref[16:, :]
     mixed_ref[0:16, :] = jnp.concatenate([top, first_ref[0:16, :].astype(F32)[8:16]], axis=0).astype(BF16)
-    share = lax.dot_general(
+    share_ref[...] = lax.dot_general(
         mixed_ref[...], pw_ref[...], (((1,), (1,)), ((), ())), preferred_element_type=F32
-    ).astype(BF16)
-    pairs = share.shape[0] // 32
-    for to in range(2 * pairs):
-        at = 16 * ((to % 2) * pairs + to // 2)
-        part_ref[16 * to : 16 * (to + 1), :] = share[at : at + 16, :]
-
-
-def project(first, head, halo, weight, bias, weight_t):
+    )
+    half = send_ref.shape[0]
+    theirs = pl.multiple_of((1 - place_ref[2]) * half, half)
+    send_ref[...] = share_ref[pl.ds(theirs, half), :].astype(BF16)
+
+
+def project(place, first, head, halo, weight, bias, weight_t):
     rows, width = first.shape
+    columns = weight_t.shape[0]
     return pl.pallas_call(
         project_kernel,
         out_shape=(
             pltpu.VMEM((rows, width), BF16),
-            jax.ShapeDtypeStruct((rows, weight_t.shape[0]), BF16),
+            pltpu.VMEM((rows, columns), F32),
+            jax.ShapeDtypeStruct((rows // 2, columns), BF16),
         ),
-        in_specs=[VMEM] * 6,
-        out_specs=(VMEM,) * 2,
+        in_specs=[SMEM] + [VMEM] * 6,
+        out_specs=(VMEM,) * 3,
         scratch_shapes=[pltpu.VMEM((16, width), F32)],
         compiler_params=params(8),
         name="project",
-    )(first, head, halo, weight, bias, weight_t)
+    )(place, first, head, halo, weight, bias, weight_t)
+
+
+def pair_kernel(place_ref, share_ref, got_ref, out_ref):
+    half = out_ref.shape[0]
+    ours = pl.multiple_of(place_ref[2] * half, half)
+    theirs = pl.multiple_of((1 - place_ref[2]) * half, half)
+    out_ref[...] = (share_ref[pl.ds(ours, half), :] + got_ref[pl.ds(theirs, half), :].astype(F32)).astype(BF16)
+
+
+def pair(place, share, got):
+    return pl.pallas_call(
+        pair_kernel,
+        out_shape=jax.ShapeDtypeStruct((share.shape[0] // 2, share.shape[1]), BF16),
+        in_specs=[SMEM] + [VMEM] * 2,
+        out_specs=VMEM,
+        compiler_params=params(8),
+        name="pair",
+    )(place, share, got)
 
 
 def total_kernel(parts_ref, out_ref):
@@ -145,7 +167,7 @@
 def total(parts):
     return pl.pallas_call(
         total_kernel,
-        out_shape=jax.ShapeDtypeStruct((parts.shape[0] // 2, parts.shape[1]), BF16),
+        out_shape=jax.ShapeDtypeStruct(parts.shape, BF16),
         in_specs=[VMEM],
         out_specs=VMEM,
         compiler_params=params(8),
@@ -190,7 +212,9 @@
     for c in range(0, width, 256):
         pre = jnp.dot(low, dtw_ref[:, c : c + 256], preferred_element_type=F32)
         pre = pre + dtb_ref[:, c : c + 256]
-        dt = jnp.maximum(pre, 0.0) + jnp.log1p(jnp.exp(-jnp.abs(pre)))
+        small = jnp.exp(-jnp.abs(pre))
+        log1p = jnp.where(small < 1e-3, small - 0.5 * small * small, jnp.log(1.0 + small))
+        dt = jnp.maximum(pre, 0.0) + log1p
         dx = dt * mixed_ref[:, c : c + 256].astype(F32)
         for h in range(2):
             at = pl.ds(c // LANES + h, rows, TILES)
@@ -326,7 +350,7 @@
             pltpu.VMEM((STATE * TILES, LANES), F32),
             pltpu.VMEM((TILES, LANES), F32),
         ),
-        in_specs=[pl.BlockSpec(memory_space=pltpu.SMEM), VMEM, VMEM],
+        in_specs=[SMEM, VMEM, VMEM],
         out_specs=(VMEM,) * 3,
         compiler_params=params(8),
         name="merge",
@@ -386,7 +410,7 @@
     on_y = [[2 * y + core for y in range(y_size)] for core in range(2)]
     on_chip = [[2 * y, 2 * y + 1] for y in range(y_size)]
     me = lax.axis_index("seq")
-    place = jnp.stack([me % Z, me // Z]).astype(jnp.int32)
+    place = jnp.stack([me % Z, me // Z, lax.axis_index("mp") % 2]).astype(jnp.int32)
     halo = lax.ppermute(inputs[rows - 8 :], "seq", [(s, s + 1) for s in range(seq - 1)])
     first, head, taps_in, bias, weight, dtw, dtb, rate, gain = mix(
         inputs,
@@ -398,8 +422,9 @@
         jnp.transpose(decay_rate),
         skip_gain.reshape(1, width),
     )
-    mixed, part = project(first, head, halo, taps_in, bias, weight)
-    parts = lax.all_to_all(part, "mp", 0, 0, tiled=True)
+    mixed, share, theirs = project(place, first, head, halo, taps_in, bias, weight)
+    both = lax.all_gather(theirs, "mp", axis=0, tiled=True, axis_index_groups=on_chip)
+    parts = lax.all_to_all(pair(place, share, both), "mp", 0, 0, tiled=True, axis_index_groups=on_y)
     mine = lax.all_to_all(total(parts), "mp", 0, 0, tiled=True, axis_index_groups=on_y)
     projected = lax.all_gather(mine, "mp", axis=0, tiled=True, axis_index_groups=on_chip)
     dt, ends = state(projected, dtw, dtb, mixed, rate)

time: 86.4 us -> 84.9 us (0.983)
  blocking collectives: 44.4 us -> 42.1 us
    all_to_all x1, blocking collectives: 19.4 us -> 17 us  [shards(): lax.all_to_all(pair(place, share, both), 'mp', 0, 0, tiled=True, axis_ind...]
    all_gather x0 -> x1, blocking collectives: none -> 2.04 us  [shards(): lax.all_gather(theirs, 'mp', axis=0, tiled=True, axis_index_groups=on_chip)]
    all_to_all x1, blocking collectives: 13.7 us -> 11.8 us  [shards(): lax.all_to_all(total(parts), 'mp', 0, 0, tiled=True, axis_index_groups=on_y)]
where the time goes in v1:
time: 84.9 us; the launch traced here: 84.4 us
  blocking collectives  42.1 us (50%)
  Pallas kernels  19 us (22%)
  waiting for transfers between devices  12.5 us (15%)
  starting transfers between devices  8.77 us (10%)
  local copies, waits for them, and re-layouts  1.94 us (2%)
    all_to_all x1, blocking collectives, shards(): lax.all_to_all(pair(place, share, both), 'mp', 0, 0, tiled=True, axis_ind...  17 us
    all_to_all x1, blocking collectives, shards(): lax.all_to_all(total(parts), 'mp', 0, 0, tiled=True, axis_index_groups=on_y)  11.8 us
    all_to_all x1, blocking collectives, shards(): got = lax.all_to_all(ends, 'seq', 0, 0, tiled=True, axis_index_groups=on_x)  9.23 us
    all_to_all x1, waiting for transfers between devices, shards(): got = lax.all_to_all(ends, 'seq', 0, 0, tiled=True, axis_index_groups=on_z)  6.54 us
    ppermute x1, waiting for transfers between devices, shards(): lax.ppermute(inputs[rows - 8:], 'seq', [(s, s + 1) for s in range(seq - 1)])  5.91 us
    pallas_call x1, Pallas kernels, local(): pl.pallas_call(local_kernel, out_shape=(flat, flat, pltpu.VMEM(rate.shape...  5.11 us
    pallas_call x1, Pallas kernels, state(): pl.pallas_call(state_kernel, out_shape=(pltpu.HBM((rows * TILES, LANES),...  4.69 us
    all_to_all x1, starting transfers between devices, shards(): got = lax.all_to_all(ends, 'seq', 0, 0, tiled=True, axis_index_groups=on_z)  4.5 us
  transfers between devices with their start and end apart: 2, of which 2 were waited for; matrix products, arithmetic and copies ran while one was open for 0% of the time, Pallas kernels for 9%

profile of v1, /device:TPU:2, one launch (start us, length us, event | category | flops | bytes accessed | tf_op | source)
XLA Modules:
  0.0 84.4 jit_solution(5846862619751921321)
XLA Ops:
  0.0 0.7 slice.3
  0.7 4.3 %collective-permute-start = (bf16[8,1024]{1,0:T(8,128)(2,1)S(1)}, bf16[8,1024]{1,0:T(8,128)(2,1)S(1)}, u32[]{:S(2)}, u32[]{:S(2)}) collective-permute-start(bf16[8,1024]{1,0:T(8,128)(2,1)S(1)} %slice.3), channel_id=1, source_target_pairs={{0,16},{16,32},{32,48},{48,64},{64,80},{80,96},{96,112},{112,128},... | collective-permute-start | bytes 49160 | tf_op jit(solution)/shard_map/ppermute | solution.py:414
  5.0 0.1 pad_add_fusion.place_ref
  5.1 2.3 %mix.1 = (bf16[256,1024]{1,0:T(8,128)(2,1)S(1)}, f32[8,1024]{1,0:T(8,128)S(1)}, f32[4,1024]{1,0:T(4,128)S(1)}, f32[1,1024]{1,0:T(1,128)S(1)}, bf16[544,1024]{1,0...) custom-call(bf16[256,1024]{1,0:T(8,128)(2,1)} %x_hbm.1, ...), custom_call_target="tpu_custom_call" | custom-call | flops 20000000 | bytes 5000000 | tf_op jit(solution)/shard_map/mix/pallas_call | solution.py:78
  7.4 5.9 %collective-permute-done.halo_ref = bf16[8,1024]{1,0:T(8,128)(2,1)S(1)} collective-permute-done((bf16[8,1024]{1,0:T(8,128)(2,1)S(1)}, bf16[8,1024]{1,0:T(8,128)(2,1)S(1)}, u32[]{:S(2)}, u32[]{:S(2)}) %collective-permute-start) | collective-permute-done | bytes 16416 | tf_op jit(solution)/shard_map/ppermute | solution.py:414
  13.3 1.2 %project.1 = (bf16[256,1024]{1,0:T(8,128)(2,1)S(1)}, f32[256,544]{1,0:T(8,128)S(1)}, bf16[128,544]{1,0:T(8,128)(2,1)S(1)}) custom-call(s32[3]{0:T(128)S(1)} %pad_add_fusion.place_ref, bf16[256,1024]{1,0:T(8,128)(2,1)S(1)} %get-tuple-element.25.first_ref, f32[8,1024]{1,0:T(8,128)S(1)} %get-tuple-element.26.head_ref, ...), custom_call_target="tpu_custom_call" | custom-call | tf_op jit(solution)/shard_map/project/pallas_call | solution.py:125
  14.5 2.0 %all_gather.6.got_ref = bf16[256,544]{1,0:T(8,128)(2,1)S(1)} all-gather(bf16[128,544]{1,0:T(8,128)(2,1)S(1)} %get-tuple-element.31), channel_id=1, replica_groups={{0,1},{2,3},{4,5},{6,7},{8,9},{10,11},{12,13},{14,15},{16,17},{18,19},{..., dimensions={0}, use_global_device_ids=true | all-gather | bytes 417792 | tf_op jit(solution)/shard_map/all_gather | solution.py:426
  16.6 0.6 pair.1
  17.2 17.0 %all_to_all.45 = bf16[8,16,544]{2,1,0:T(8,128)(2,1)S(1)} all-to-all(bf16[8,16,544]{2,1,0:T(8,128)(2,1)S(1)} %bitcast.19), channel_id=1, replica_groups={{0,2,4,6,8,10,12,14},{1,3,5,7,9,11,13,15},{16,18,20,22,24,26,28,30},{17..., dimensions={0} | all-to-all | bytes 278528 | tf_op jit(solution)/shard_map/all_to_all | solution.py:427
  34.2 11.8 %all_to_all.46 = bf16[8,16,544]{2,1,0:T(8,128)(2,1)S(1)} all-to-all(bf16[8,16,544]{2,1,0:T(8,128)(2,1)S(1)} %bitcast.18), channel_id=1, replica_groups={{0,2,4,6,8,10,12,14},{1,3,5,7,9,11,13,15},{16,18,20,22,24,26,28,30},{17..., dimensions={0} | all-to-all | bytes 278528 | tf_op jit(solution)/shard_map/all_to_all | solution.py:428
  46.0 2.0 %all_gather.7.g_ref = bf16[256,544]{1,0:T(8,128)(2,1)S(1)} all-gather(bf16[128,544]{1,0:T(8,128)(2,1)S(1)} %bitcast.22), channel_id=1, replica_groups={{0,1},{2,3},{4,5},{6,7},{8,9},{10,11},{12,13},{14,15},{16,17},{18,19},{..., dimensions={0}, use_global_device_ids=true | all-gather | bytes 417792 | tf_op jit(solution)/shard_map/all_gather | solution.py:429
  48.0 4.7 %state.1 = (f32[2048,128]{1,0:T(8,128)}, bf16[1152,128]{1,0:T(8,128)(2,1)}) custom-call(bf16[256,544]{1,0:T(8,128)(2,1)S(1)} %all_gather.7.g_ref, bf16[512,1024]{1,0:T(8,128)(2,1)S(1)} %get-tuple-element.32.dtw_ref, f32[1,1024]{1,0:T(1,128)S(1)} %get-tuple-element.33.dtb_ref, bf16[256,1024]{1,0:T(8,128)(2,1)S(1)} %get-tuple-element.34.mixed_ref, ...), custom_call_target="tpu_custom_call" | custom-call | tf_op jit(solution)/shard_map/state/pallas_call | solution.py:251
  52.7 4.5 %all-to-all-start.2 = ((bf16[8,144,128]{2,1,0:T(8,128)(2,1)}), bf16[8,144,128]{2,1,0:T(8,128)(2,1)S(1)}, u32[]{:S(2)}, u32[]{:S(2)}) async-start(bf16[8,144,128]{2,1,0:T(8,128)(2,1)} %bitcast.12), calls=%async_computation.2 | async-start | bytes 589824 | tf_op jit(solution)/shard_map/all_to_all | solution.py:431
  57.2 0.0 copy-start
  57.2 1.2 %copy-done = f32[2048,128]{1,0:T(8,128)S(1)} copy-done((f32[2048,128]{1,0:T(8,128)S(1)}, f32[2048,128]{1,0:T(8,128)}, u32[]{:S(2)}) %copy-start) | copy-done | bytes 1048600
  58.4 5.1 %local.1 = (f32[2048,128]{1,0:T(8,128)S(1)}, f32[2048,128]{1,0:T(8,128)S(1)}, f32[128,128]{1,0:T(8,128)S(1)}) custom-call(bf16[256,544]{1,0:T(8,128)(2,1)S(1)} %all_gather.7.g_ref, f32[2048,128]{1,0:T(8,128)S(1)} %copy-done, f32[128,128]{1,0:T(8,128)S(1)} %get-tuple-element.35.rate_ref, bf16[256,1024]{1,0:T(8,128)(2,1)S(1)} %get-tuple-element.34.mixed_ref, ...), custom_call_target="tpu_custom_call" | custom-call | flops 60000000 | bytes 15000000 | tf_op jit(solution)/shard_map/local/pallas_call | solution.py:303
  63.6 6.5 %all-to-all-done.2 = bf16[8,144,128]{2,1,0:T(8,128)(2,1)S(1)} async-done(((bf16[8,144,128]{2,1,0:T(8,128)(2,1)}), bf16[8,144,128]{2,1,0:T(8,128)(2,1)S(1)}, u32[]{:S(2)}, u32[]{:S(2)}) %all-to-all-start.2) | async-done | bytes 294944 | tf_op jit(solution)/shard_map/all_to_all | solution.py:431
  70.1 0.7 merge.1
  70.8 9.2 %all_to_all.47 = bf16[4,144,128]{2,1,0:T(8,128)(2,1)S(1)} all-to-all(bf16[4,144,128]{2,1,0:T(8,128)(2,1)S(1)} %bitcast.21), channel_id=1, replica_groups={{0,128,256,384},{16,144,272,400},{32,160,288,416},{48,176,304,432},{64,..., dimensions={0} | all-to-all | bytes 294912 | tf_op jit(solution)/shard_map/all_to_all | solution.py:434
  80.0 4.4 %finish.1 = bf16[256,1024]{1,0:T(8,128)(2,1)} custom-call(bf16[576,128]{1,0:T(8,128)(2,1)S(1)} %bitcast.20, f32[128,128]{1,0:T(8,128)S(1)} %get-tuple-element.41.state_ref, f32[8,128]{1,0:T(8,128)S(1)} %get-tuple-element.42.sum_ref, f32[128,128]{1,0:T(8,128)S(1)} %get-tuple-element.39.rate_ref, bf16[256,544]{1,0:T(8,128)(2,1)S(1)} %all_gather.7.g_ref, ...), custom_call_target="tpu_custom_call" | custom-call | tf_op jit(solution)/shard_map/finish/pallas_call | solution.py:393
  (1 shorter events, 0.0 us)
Async XLA Ops:
  0.7 12.6 %collective-permute-start = (bf16[8,1024]{1,0:T(8,128)(2,1)S(1)}, bf16[8,1024]{1,0:T(8,128)(2,1)S(1)}, u32[]{:S(2)}, u32[]{:S(2)}) collective-permute-start(bf16[8,1024]{1,0:T(8,128)(2,1)S(1)} %slice.3), channel_id=1, source_target_pairs={{0,16},{16,32},{32,48},{48,64},{64,80},{80,96},{96,112},{112,128},... | collective-permute-start | bytes 49160 | tf_op jit(solution)/shard_map/ppermute | solution.py:414
  52.7 17.4 %all-to-all-start.2 = ((bf16[8,144,128]{2,1,0:T(8,128)(2,1)}), bf16[8,144,128]{2,1,0:T(8,128)(2,1)S(1)}, u32[]{:S(2)}, u32[]{:S(2)}) async-start(bf16[8,144,128]{2,1,0:T(8,128)(2,1)} %bitcast.12), calls=%async_computation.2 | async-start | bytes 589824 | tf_op jit(solution)/shard_map/all_to_all | solution.py:431
  57.2 1.2 %copy-start = (f32[2048,128]{1,0:T(8,128)S(1)}, f32[2048,128]{1,0:T(8,128)}, u32[]{:S(2)}) copy-start(f32[2048,128]{1,0:T(8,128)} %get-tuple-element.37.dt_ref) | copy-start | bytes 3145732

commit v2 on v1

--- a/solution.py
+++ b/solution.py
@@ -32,9 +32,13 @@
     return pre / (1.0 + jnp.exp(-pre))
 
 
+def multiply(rows, weight_t):
+    return lax.dot_general(rows, weight_t, (((1,), (1,)), ((), ())), preferred_element_type=F32).astype(BF16)
+
+
 def mix_kernel(
     x_hbm, w_hbm, b_hbm, pw_hbm, dtw_hbm, dtb_hbm, decay_hbm, gain_hbm,
-    mixed_ref, head_ref, w_ref, b_ref, pw_ref, dtw_ref, dtb_ref, rate_ref, gain_ref,
+    mixed_ref, head_ref, share_ref, w_ref, b_ref, pw_ref, dtw_ref, dtb_ref, rate_ref, gain_ref,
     x_ref, pad_ref, decay_ref, row_ref, sems,
 ):
     rows = x_hbm.shape[0]
@@ -71,6 +75,7 @@
         c = slice(LANES * j, LANES * (j + 1))
         rate_ref[pl.ds(j, STATE, TILES), :] = decay_ref[:, c] * -LOG2E
         gain_ref[j : j + 1, :] = row_ref[:, c]
+    share_ref[...] = multiply(mixed_ref[...], pw_ref[...])
 
 
 def mix(x, weight, bias, weight_t, dtw, dtb, decay, gain):
@@ -80,6 +85,7 @@
         out_shape=(
             pltpu.VMEM((rows, width), BF16),
             pltpu.VMEM((8, width), F32),
+            pltpu.VMEM((rows, weight_t.shape[0]), BF16),
             pltpu.VMEM(weight.shape, F32),
             pltpu.VMEM(bias.shape, F32),
             pltpu.VMEM(weight_t.shape, BF16),
@@ -89,7 +95,7 @@
             pltpu.VMEM((TILES, LANES), F32),
         ),
         in_specs=[pl.BlockSpec(memory_space=pltpu.HBM)] * 8,
-        out_specs=(VMEM,) * 9,
+        out_specs=(VMEM,) * 10,
         scratch_shapes=[
             pltpu.VMEM((rows, width), BF16),
             pltpu.VMEM((rows + 8, width), F32),
@@ -104,55 +110,51 @@
 
 
 def project_kernel(
-    place_ref, first_ref, head_ref, halo_ref, w_ref, b_ref, pw_ref, mixed_ref, share_ref, send_ref, pad_ref
+    place_ref, first_ref, head_ref, share_ref, halo_ref, w_ref, b_ref, pw_ref, mixed_ref, ours_ref, theirs_ref, pad_ref, all_ref
 ):
     pad_ref[0:8, :] = halo_ref[...].astype(F32)
     pad_ref[8:16, :] = head_ref[...]
     top = taps(pad_ref, w_ref, b_ref, 0, 8)
+    top = jnp.concatenate([top, first_ref[0:16, :].astype(F32)[8:16]], axis=0).astype(BF16)
     mixed_ref[16:, :] = first_ref[16:, :]
-    mixed_ref[0:16, :] = jnp.concatenate([top, first_ref[0:16, :].astype(F32)[8:16]], axis=0).astype(BF16)
-    share_ref[...] = lax.dot_general(
-        mixed_ref[...], pw_ref[...], (((1,), (1,)), ((), ())), preferred_element_type=F32
-    )
-    half = send_ref.shape[0]
-    theirs = pl.multiple_of((1 - place_ref[2]) * half, half)
-    send_ref[...] = share_ref[pl.ds(theirs, half), :].astype(BF16)
-
-
-def project(place, first, head, halo, weight, bias, weight_t):
+    mixed_ref[0:16, :] = top
+    all_ref[16:, :] = share_ref[16:, :]
+    all_ref[0:16, :] = multiply(top, pw_ref[...])
+    half = ours_ref.shape[0]
+    core = place_ref[2]
+    ours_ref[...] = all_ref[pl.ds(pl.multiple_of(core * half, half), half), :]
+    theirs_ref[...] = all_ref[pl.ds(pl.multiple_of((1 - core) * half, half), half), :]
+
+
+def project(place, first, head, share, halo, weight, bias, weight_t):
     rows, width = first.shape
-    columns = weight_t.shape[0]
+    half = pltpu.VMEM((rows // 2, share.shape[1]), BF16)
     return pl.pallas_call(
         project_kernel,
-        out_shape=(
-            pltpu.VMEM((rows, width), BF16),
-            pltpu.VMEM((rows, columns), F32),
-            jax.ShapeDtypeStruct((rows // 2, columns), BF16),
-        ),
-        in_specs=[SMEM] + [VMEM] * 6,
+        out_shape=(pltpu.VMEM((rows, width), BF16), half, half),
+        in_specs=[SMEM] + [VMEM] * 7,
         out_specs=(VMEM,) * 3,
-        scratch_shapes=[pltpu.VMEM((16, width), F32)],
+        scratch_shapes=[pltpu.VMEM((16, width), F32), pltpu.VMEM(share.shape, BF16)],
         compiler_params=params(8),
         name="project",
-    )(place, first, head, halo, weight, bias, weight_t)
-
-
-def pair_kernel(place_ref, share_ref, got_ref, out_ref):
+    )(place, first, head, share, halo, weight, bias, weight_t)
+
+
+def pair_kernel(place_ref, ours_ref, got_ref, out_ref):
     half = out_ref.shape[0]
-    ours = pl.multiple_of(place_ref[2] * half, half)
     theirs = pl.multiple_of((1 - place_ref[2]) * half, half)
-    out_ref[...] = (share_ref[pl.ds(ours, half), :] + got_ref[pl.ds(theirs, half), :].astype(F32)).astype(BF16)
-
-
-def pair(place, share, got):
+    out_ref[...] = (ours_ref[...].astype(F32) + got_ref[pl.ds(theirs, half), :].astype(F32)).astype(BF16)
+
+
+def pair(place, ours, got):
     return pl.pallas_call(
         pair_kernel,
-        out_shape=jax.ShapeDtypeStruct((share.shape[0] // 2, share.shape[1]), BF16),
+        out_shape=jax.ShapeDtypeStruct(ours.shape, BF16),
         in_specs=[SMEM] + [VMEM] * 2,
         out_specs=VMEM,
         compiler_params=params(8),
         name="pair",
-    )(place, share, got)
+    )(place, ours, got)
 
 
 def total_kernel(parts_ref, out_ref):
@@ -252,7 +254,7 @@
         state_kernel,
         out_shape=(
             pltpu.HBM((rows * TILES, LANES), F32),
-            jax.ShapeDtypeStruct((Z * PACK, LANES), BF16),
+            pltpu.VMEM((Z * PACK, LANES), BF16),
         ),
         in_specs=[VMEM] * 5,
         out_specs=(pl.BlockSpec(memory_space=pltpu.HBM), VMEM),
@@ -357,8 +359,8 @@
     )(place, got, rate)
 
 
-def finish_kernel(got_ref, state_ref, sum_ref, rate_ref, g_ref, y_ref, cum_ref, out_ref, tot_ref, bc_ref):
-    rows = out_ref.shape[0]
+def finish_kernel(got_ref, state_ref, sum_ref, rate_ref, g_ref, y_ref, cum_ref, out_hbm, tot_ref, bc_ref, out_ref, sems):
+    rows = out_hbm.shape[0]
     spread(g_ref[:, DT_RANK : DT_RANK + 2 * STATE].astype(F32), STATE, STATE, bc_ref)
     count = got_ref.shape[0] // PACK - 1
     sums = [sums_of(got_ref, k) for k in range(count)]
@@ -383,9 +385,25 @@
             tot_ref[token(t), :] = y
         return carry
 
-    lax.fori_loop(0, rows // UNROLL, group, tuple(incoming))
-    for j in range(TILES):
-        out_ref[:, LANES * j : LANES * (j + 1)] = tot_ref[pl.ds(j, rows, TILES), :].astype(BF16)
+    pieces = sems.shape[0]
+    some = rows // pieces
+
+    def leave(i):
+        at = pl.ds(pl.multiple_of(i * some, some), some)
+        return pltpu.make_async_copy(out_ref.at[at], out_hbm.at[at], sems.at[i])
+
+    def piece(i, carry):
+        lax.fori_loop(i * (some // UNROLL), (i + 1) * (some // UNROLL), group, carry)
+        at = pl.ds(pl.multiple_of(i * some, some), some)
+        for j in range(TILES):
+            rows_j = tot_ref[pl.ds(i * (some * TILES) + j, some, TILES), :]
+            out_ref[at, LANES * j : LANES * (j + 1)] = rows_j.astype(BF16)
+        leave(i).start()
+        return carry
+
+    lax.fori_loop(0, pieces, piece, tuple(incoming))
+    for i in range(pieces):
+        leave(i).wait()
 
 
 def finish(got, states, sums, rate, g, y, cum):
@@ -394,8 +412,13 @@
         finish_kernel,
         out_shape=jax.ShapeDtypeStruct((rows, TILES * LANES), BF16),
         in_specs=[VMEM] * 7,
-        out_specs=VMEM,
-        scratch_shapes=[pltpu.VMEM(y.shape, F32), pltpu.VMEM((STATE, rows, LANES), F32)],
+        out_specs=pl.BlockSpec(memory_space=pltpu.HBM),
+        scratch_shapes=[
+            pltpu.VMEM(y.shape, F32),
+            pltpu.VMEM((STATE, rows, LANES), F32),
+            pltpu.VMEM((rows, TILES * LANES), BF16),
+            pltpu.SemaphoreType.DMA((4,)),
+        ],
         compiler_params=params(8),
         name="finish",
     )(got, states, sums, rate, g, y, cum)
@@ -412,7 +435,7 @@
     me = lax.axis_index("seq")
     place = jnp.stack([me % Z, me // Z, lax.axis_index("mp") % 2]).astype(jnp.int32)
     halo = lax.ppermute(inputs[rows - 8 :], "seq", [(s, s + 1) for s in range(seq - 1)])
-    first, head, taps_in, bias, weight, dtw, dtb, rate, gain = mix(
+    first, head, share, taps_in, bias, weight, dtw, dtb, rate, gain = mix(
         inputs,
         conv_weight,
         conv_bias.reshape(1, width),
@@ -422,9 +445,9 @@
         jnp.transpose(decay_rate),
         skip_gain.reshape(1, width),
     )
-    mixed, share, theirs = project(place, first, head, halo, taps_in, bias, weight)
+    mixed, ours, theirs = project(place, first, head, share, halo, taps_in, bias, weight)
     both = lax.all_gather(theirs, "mp", axis=0, tiled=True, axis_index_groups=on_chip)
-    parts = lax.all_to_all(pair(place, share, both), "mp", 0, 0, tiled=True, axis_index_groups=on_y)
+    parts = lax.all_to_all(pair(place, ours, both), "mp", 0, 0, tiled=True, axis_index_groups=on_y)
     mine = lax.all_to_all(total(parts), "mp", 0, 0, tiled=True, axis_index_groups=on_y)
     projected = lax.all_gather(mine, "mp", axis=0, tiled=True, axis_index_groups=on_chip)
     dt, ends = state(projected, dtw, dtb, mixed, rate)

time: 84.9 us -> 84.6 us (level)
  transfers between devices with their start and end apart: 2 -> 2, of which waited for: 2 -> 2; matrix products, arithmetic and copies ran while one was open for 0% -> 0% of each run, Pallas kernels for 9% -> 10%
where the time goes in v2:
time: 84.6 us; the launch traced here: 84.1 us
  blocking collectives  42.1 us (50%)
  Pallas kernels  19.3 us (23%)
  waiting for transfers between devices  11.8 us (14%)
  starting transfers between devices  8.78 us (10%)
  local copies, waits for them, and re-layouts  1.94 us (2%)
    all_to_all x1, blocking collectives, shards(): lax.all_to_all(pair(place, ours, both), 'mp', 0, 0, tiled=True, axis_inde...  17 us
    all_to_all x1, blocking collectives, shards(): lax.all_to_all(total(parts), 'mp', 0, 0, tiled=True, axis_index_groups=on_y)  11.8 us
    all_to_all x1, blocking collectives, shards(): got = lax.all_to_all(ends, 'seq', 0, 0, tiled=True, axis_index_groups=on_x)  9.23 us
    all_to_all x1, waiting for transfers between devices, shards(): got = lax.all_to_all(ends, 'seq', 0, 0, tiled=True, axis_index_groups=on_z)  6.55 us
    ppermute x1, waiting for transfers between devices, shards(): lax.ppermute(inputs[rows - 8:], 'seq', [(s, s + 1) for s in range(seq - 1)])  5.3 us
    pallas_call x1, Pallas kernels, local(): pl.pallas_call(local_kernel, out_shape=(flat, flat, pltpu.VMEM(rate.shape...  5.11 us
    pallas_call x1, Pallas kernels, state(): pl.pallas_call(state_kernel, out_shape=(pltpu.HBM((rows * TILES, LANES),...  4.68 us
    all_to_all x1, starting transfers between devices, shards(): got = lax.all_to_all(ends, 'seq', 0, 0, tiled=True, axis_index_groups=on_z)  4.51 us
  transfers between devices with their start and end apart: 2, of which 2 were waited for; matrix products, arithmetic and copies ran while one was open for 0% of the time, Pallas kernels for 10%

profile of v2, /device:TPU:2, one launch (start us, length us, event | category | flops | bytes accessed | tf_op | source)
XLA Modules:
  0.0 84.1 jit_solution(4453411922707532045)
XLA Ops:
  0.0 0.7 slice.3
  0.7 4.3 %collective-permute-start = (bf16[8,1024]{1,0:T(8,128)(2,1)S(1)}, bf16[8,1024]{1,0:T(8,128)(2,1)S(1)}, u32[]{:S(2)}, u32[]{:S(2)}) collective-permute-start(bf16[8,1024]{1,0:T(8,128)(2,1)S(1)} %slice.3), channel_id=1, source_target_pairs={{0,16},{16,32},{32,48},{48,64},{64,80},{80,96},{96,112},{112,128},... | collective-permute-start | bytes 49160 | tf_op jit(solution)/shard_map/ppermute | solution.py:437
  5.0 0.1 pad_add_fusion.place_ref
  5.1 2.9 %mix.1 = (bf16[256,1024]{1,0:T(8,128)(2,1)S(1)}, f32[8,1024]{1,0:T(8,128)S(1)}, bf16[256,544]{1,0:T(8,128)(2,1)S(1)}, f32[4,1024]{1,0:T(4,128)S(1)}, f32[1,1024]...) custom-call(bf16[256,1024]{1,0:T(8,128)(2,1)} %x_hbm.1, ...), custom_call_target="tpu_custom_call" | custom-call | flops 20000000 | bytes 5000000 | tf_op jit(solution)/shard_map/mix/pallas_call | solution.py:83
  8.0 5.3 %collective-permute-done.halo_ref = bf16[8,1024]{1,0:T(8,128)(2,1)S(1)} collective-permute-done((bf16[8,1024]{1,0:T(8,128)(2,1)S(1)}, bf16[8,1024]{1,0:T(8,128)(2,1)S(1)}, u32[]{:S(2)}, u32[]{:S(2)}) %collective-permute-start) | collective-permute-done | bytes 16416 | tf_op jit(solution)/shard_map/ppermute | solution.py:437
  13.3 1.0 %project.1 = (bf16[256,1024]{1,0:T(8,128)(2,1)S(1)}, bf16[128,544]{1,0:T(8,128)(2,1)S(1)}, bf16[128,544]{1,0:T(8,128)(2,1)S(1)}) custom-call(s32[3]{0:T(128)S(1)} %pad_add_fusion.place_ref, bf16[256,1024]{1,0:T(8,128)(2,1)S(1)} %get-tuple-element.26.first_ref, f32[8,1024]{1,0:T(8,128)S(1)} %get-tuple-element.27.head_ref, ...), custom_call_target="tpu_custom_call" | custom-call | tf_op jit(solution)/shard_map/project/pallas_call | solution.py:132
  14.4 2.0 %all_gather.6.got_ref = bf16[256,544]{1,0:T(8,128)(2,1)S(1)} all-gather(bf16[128,544]{1,0:T(8,128)(2,1)S(1)} %get-tuple-element.33), channel_id=1, replica_groups={{0,1},{2,3},{4,5},{6,7},{8,9},{10,11},{12,13},{14,15},{16,17},{18,19},{..., dimensions={0}, use_global_device_ids=true | all-gather | bytes 417792 | tf_op jit(solution)/shard_map/all_gather | solution.py:449
  16.4 0.6 pair.1
  17.0 17.0 %all_to_all.45 = bf16[8,16,544]{2,1,0:T(8,128)(2,1)S(1)} all-to-all(bf16[8,16,544]{2,1,0:T(8,128)(2,1)S(1)} %bitcast.19), channel_id=1, replica_groups={{0,2,4,6,8,10,12,14},{1,3,5,7,9,11,13,15},{16,18,20,22,24,26,28,30},{17..., dimensions={0} | all-to-all | bytes 278528 | tf_op jit(solution)/shard_map/all_to_all | solution.py:450
  34.0 11.8 %all_to_all.46 = bf16[8,16,544]{2,1,0:T(8,128)(2,1)S(1)} all-to-all(bf16[8,16,544]{2,1,0:T(8,128)(2,1)S(1)} %bitcast.18), channel_id=1, replica_groups={{0,2,4,6,8,10,12,14},{1,3,5,7,9,11,13,15},{16,18,20,22,24,26,28,30},{17..., dimensions={0} | all-to-all | bytes 278528 | tf_op jit(solution)/shard_map/all_to_all | solution.py:451
  45.8 2.0 %all_gather.7.g_ref = bf16[256,544]{1,0:T(8,128)(2,1)S(1)} all-gather(bf16[128,544]{1,0:T(8,128)(2,1)S(1)} %bitcast.22), channel_id=1, replica_groups={{0,1},{2,3},{4,5},{6,7},{8,9},{10,11},{12,13},{14,15},{16,17},{18,19},{..., dimensions={0}, use_global_device_ids=true | all-gather | bytes 417792 | tf_op jit(solution)/shard_map/all_gather | solution.py:452
  47.9 4.7 %state.1 = (f32[2048,128]{1,0:T(8,128)}, bf16[1152,128]{1,0:T(8,128)(2,1)}) custom-call(bf16[256,544]{1,0:T(8,128)(2,1)S(1)} %all_gather.7.g_ref, bf16[512,1024]{1,0:T(8,128)(2,1)S(1)} %get-tuple-element.34.dtw_ref, f32[1,1024]{1,0:T(1,128)S(1)} %get-tuple-element.35.dtb_ref, bf16[256,1024]{1,0:T(8,128)(2,1)S(1)} %get-tuple-element.36.mixed_ref, ...), custom_call_target="tpu_custom_call" | custom-call | tf_op jit(solution)/shard_map/state/pallas_call | solution.py:253
  52.6 4.5 %all-to-all-start.2 = ((bf16[8,144,128]{2,1,0:T(8,128)(2,1)}), bf16[8,144,128]{2,1,0:T(8,128)(2,1)S(1)}, u32[]{:S(2)}, u32[]{:S(2)}) async-start(bf16[8,144,128]{2,1,0:T(8,128)(2,1)} %bitcast.12), calls=%async_computation.2 | async-start | bytes 589824 | tf_op jit(solution)/shard_map/all_to_all | solution.py:454
  57.1 0.0 copy-start
  57.1 1.2 %copy-done = f32[2048,128]{1,0:T(8,128)S(1)} copy-done((f32[2048,128]{1,0:T(8,128)S(1)}, f32[2048,128]{1,0:T(8,128)}, u32[]{:S(2)}) %copy-start) | copy-done | bytes 1048600
  58.3 5.1 %local.1 = (f32[2048,128]{1,0:T(8,128)S(1)}, f32[2048,128]{1,0:T(8,128)S(1)}, f32[128,128]{1,0:T(8,128)S(1)}) custom-call(bf16[256,544]{1,0:T(8,128)(2,1)S(1)} %all_gather.7.g_ref, f32[2048,128]{1,0:T(8,128)S(1)} %copy-done, f32[128,128]{1,0:T(8,128)S(1)} %get-tuple-element.37.rate_ref, bf16[256,1024]{1,0:T(8,128)(2,1)S(1)} %get-tuple-element.36.mixed_ref, ...), custom_call_target="tpu_custom_call" | custom-call | flops 60000000 | bytes 15000000 | tf_op jit(solution)/shard_map/local/pallas_call | solution.py:305
  63.4 6.5 %all-to-all-done.2 = bf16[8,144,128]{2,1,0:T(8,128)(2,1)S(1)} async-done(((bf16[8,144,128]{2,1,0:T(8,128)(2,1)}), bf16[8,144,128]{2,1,0:T(8,128)(2,1)S(1)}, u32[]{:S(2)}, u32[]{:S(2)}) %all-to-all-start.2) | async-done | bytes 294944 | tf_op jit(solution)/shard_map/all_to_all | solution.py:454
  70.0 0.7 merge.1
  70.6 9.2 %all_to_all.47 = bf16[4,144,128]{2,1,0:T(8,128)(2,1)S(1)} all-to-all(bf16[4,144,128]{2,1,0:T(8,128)(2,1)S(1)} %bitcast.21), channel_id=1, replica_groups={{0,128,256,384},{16,144,272,400},{32,160,288,416},{48,176,304,432},{64,..., dimensions={0} | all-to-all | bytes 294912 | tf_op jit(solution)/shard_map/all_to_all | solution.py:457
  79.9 4.3 %finish.1 = bf16[256,1024]{1,0:T(8,128)(2,1)} custom-call(bf16[576,128]{1,0:T(8,128)(2,1)S(1)} %bitcast.20, f32[128,128]{1,0:T(8,128)S(1)} %get-tuple-element.43.state_ref, f32[8,128]{1,0:T(8,128)S(1)} %get-tuple-element.44.sum_ref, f32[128,128]{1,0:T(8,128)S(1)} %get-tuple-element.41.rate_ref, bf16[256,544]{1,0:T(8,128)(2,1)S(1)} %all_gather.7.g_ref, ...), custom_call_target="tpu_custom_call" | custom-call | tf_op jit(solution)/shard_map/finish/pallas_call | solution.py:411
  (1 shorter events, 0.0 us)
Async XLA Ops:
  0.7 12.6 %collective-permute-start = (bf16[8,1024]{1,0:T(8,128)(2,1)S(1)}, bf16[8,1024]{1,0:T(8,128)(2,1)S(1)}, u32[]{:S(2)}, u32[]{:S(2)}) collective-permute-start(bf16[8,1024]{1,0:T(8,128)(2,1)S(1)} %slice.3), channel_id=1, source_target_pairs={{0,16},{16,32},{32,48},{48,64},{64,80},{80,96},{96,112},{112,128},... | collective-permute-start | bytes 49160 | tf_op jit(solution)/shard_map/ppermute | solution.py:437
  52.6 17.4 %all-to-all-start.2 = ((bf16[8,144,128]{2,1,0:T(8,128)(2,1)}), bf16[8,144,128]{2,1,0:T(8,128)(2,1)S(1)}, u32[]{:S(2)}, u32[]{:S(2)}) async-start(bf16[8,144,128]{2,1,0:T(8,128)(2,1)} %bitcast.12), calls=%async_computation.2 | async-start | bytes 589824 | tf_op jit(solution)/shard_map/all_to_all | solution.py:454
  57.1 1.2 %copy-start = (f32[2048,128]{1,0:T(8,128)S(1)}, f32[2048,128]{1,0:T(8,128)}, u32[]{:S(2)}) copy-start(f32[2048,128]{1,0:T(8,128)} %get-tuple-element.39.dt_ref) | copy-start | bytes 3145732

commit v3 on v2

--- a/solution.py
+++ b/solution.py
@@ -270,33 +270,61 @@
 
 
 def local_kernel(
-    g_ref, dt_ref, rate_ref, mixed_ref, gain_ref, y_ref, cum_ref, rate_out, x_ref, bc_ref
+    g_ref, dt_ref, rate_ref, mixed_ref, gain_ref, y_ref, e_hbm, rate_out, x_ref, bc_ref, e_ref, sems
 ):
     rows = mixed_ref.shape[0]
+    chunk = e_ref.shape[1] // (STATE * TILES)
     rate_out[...] = rate_ref[...]
     spread(g_ref[:, DT_RANK : DT_RANK + 2 * STATE].astype(F32), 0, 2 * STATE, bc_ref)
     for j in range(TILES):
         x_ref[pl.ds(j, rows, TILES), :] = mixed_ref[:, LANES * j : LANES * (j + 1)].astype(F32)
 
-    def group(i, carry):
-        states, total = list(carry[:STATE]), carry[STATE]
-        t0 = pl.multiple_of(i * UNROLL, UNROLL)
-        for r in range(UNROLL):
-            t = t0 + r
-            dt, x = dt_ref[token(t), :], x_ref[token(t), :]
-            dx, y = dt * x, gain_ref[...] * x
-            total = total + dt
-            cum_ref[token(t), :] = total
-            for n in range(STATE):
-                enter = jnp.broadcast_to(bc_ref[n, pl.ds(t, 1), :], dt.shape)
-                read = jnp.broadcast_to(bc_ref[STATE + n, pl.ds(t, 1), :], dt.shape)
-                states[n] = jnp.exp2(dt * rate_ref[tile(n), :]) * states[n] + dx * enter
-                y = y + states[n] * read
-            y_ref[token(t), :] = y
-        return (*states, total)
+    def leave(i, slot):
+        size = chunk * STATE * TILES
+        at = pl.ds(pl.multiple_of(i * size, size), size)
+        return pltpu.make_async_copy(e_ref.at[slot], e_hbm.at[at], sems.at[slot])
+
+    def group(first, slot):
+        def one(i, carry):
+            states, total = list(carry[:STATE]), carry[STATE]
+            t0 = pl.multiple_of(i * UNROLL, UNROLL)
+            for r in range(UNROLL):
+                t = first + t0 + r
+                dt, x = dt_ref[token(t), :], x_ref[token(t), :]
+                dx, y = dt * x, gain_ref[...] * x
+                total = total + dt
+                weights = []
+                for n in range(STATE):
+                    enter = jnp.broadcast_to(bc_ref[n, pl.ds(t, 1), :], dt.shape)
+                    read = jnp.broadcast_to(bc_ref[STATE + n, pl.ds(t, 1), :], dt.shape)
+                    states[n] = jnp.exp2(dt * rate_ref[tile(n), :]) * states[n] + dx * enter
+                    y = y + states[n] * read
+                    weights.append(jnp.exp2(total * rate_ref[tile(n), :]) * read)
+                    if n % 2:
+                        at = (t0 + r) * (STATE * TILES) + TILES * (n - 1)
+                        both = jnp.concatenate(weights[n - 1 :], axis=0).astype(BF16)
+                        e_ref[slot, pl.ds(pl.multiple_of(at, 2 * TILES), 2 * TILES), :] = both
+                y_ref[token(t), :] = y
+            return (*states, total)
+
+        return one
+
+    def piece(i, carry):
+        slot = lax.rem(i, 2)
+
+        @pl.when(i >= 2)
+        def _():
+            leave(i - 2, slot).wait()
+
+        carry = lax.fori_loop(0, chunk // UNROLL, group(pl.multiple_of(i * chunk, chunk), slot), carry)
+        leave(i, slot).start()
+        return carry
 
     zero = jnp.zeros((TILES, LANES), F32)
-    lax.fori_loop(0, rows // UNROLL, group, (zero,) * (STATE + 1))
+    pieces = rows // chunk
+    lax.fori_loop(0, pieces, piece, (zero,) * (STATE + 1))
+    for i in range(pieces - 2, pieces):
+        leave(i, i % 2).wait()
 
 
 def local(g, dt, rate, mixed, gain):
@@ -304,10 +332,19 @@
     flat = pltpu.VMEM((rows * TILES, LANES), F32)
     return pl.pallas_call(
         local_kernel,
-        out_shape=(flat, flat, pltpu.VMEM(rate.shape, F32)),
+        out_shape=(
+            flat,
+            pltpu.HBM((rows * STATE * TILES, LANES), BF16),
+            pltpu.VMEM(rate.shape, F32),
+        ),
         in_specs=[VMEM] * 5,
-        out_specs=(VMEM,) * 3,
-        scratch_shapes=[flat, pltpu.VMEM((2 * STATE, rows, LANES), F32)],
+        out_specs=(VMEM, pl.BlockSpec(memory_space=pltpu.HBM), VMEM),
+        scratch_shapes=[
+            flat,
+            pltpu.VMEM((2 * STATE, rows, LANES), F32),
+            pltpu.VMEM((2, 32 * STATE * TILES, LANES), BF16),
+            pltpu.SemaphoreType.DMA((2,)),
+        ],
         compiler_params=params(12),
         cost_estimate=cost(60_000_000),
         name="local",
@@ -355,13 +392,13 @@
         in_specs=[SMEM, VMEM, VMEM],
         out_specs=(VMEM,) * 3,
         compiler_params=params(8),
+        cost_estimate=cost(100_000_000),
         name="merge",
     )(place, got, rate)
 
 
-def finish_kernel(got_ref, state_ref, sum_ref, rate_ref, g_ref, y_ref, cum_ref, out_hbm, tot_ref, bc_ref, out_ref, sems):
+def finish_kernel(got_ref, state_ref, sum_ref, rate_ref, y_ref, e_ref, out_hbm, tot_ref, out_ref, sems):
     rows = out_hbm.shape[0]
-    spread(g_ref[:, DT_RANK : DT_RANK + 2 * STATE].astype(F32), STATE, STATE, bc_ref)
     count = got_ref.shape[0] // PACK - 1
     sums = [sums_of(got_ref, k) for k in range(count)]
     incoming = []
@@ -378,11 +415,14 @@
         t0 = pl.multiple_of(i * UNROLL, UNROLL)
         for r in range(UNROLL):
             t = t0 + r
-            cum, y = cum_ref[token(t), :], y_ref[token(t), :]
-            for n in range(STATE):
-                read = jnp.broadcast_to(bc_ref[n, pl.ds(t, 1), :], cum.shape)
-                y = y + jnp.exp2(cum * rate_ref[tile(n), :]) * (carry[n] * read)
-            tot_ref[token(t), :] = y
+            more = []
+            for n in range(0, STATE, 2):
+                at = pl.multiple_of(t * STATE * TILES + n * TILES, 2 * TILES)
+                both = e_ref[pl.ds(at, 2 * TILES), :].astype(F32)
+                more.append(both[:TILES] * carry[n] + both[TILES:] * carry[n + 1])
+            while len(more) > 1:
+                more = [a + b for a, b in zip(more[::2], more[1::2])]
+            tot_ref[token(t), :] = y_ref[token(t), :] + more[0]
         return carry
 
     pieces = sems.shape[0]
@@ -406,22 +446,21 @@
         leave(i).wait()
 
 
-def finish(got, states, sums, rate, g, y, cum):
-    rows = g.shape[0]
+def finish(got, states, sums, rate, y, e):
+    rows = y.shape[0] // TILES
     return pl.pallas_call(
         finish_kernel,
         out_shape=jax.ShapeDtypeStruct((rows, TILES * LANES), BF16),
-        in_specs=[VMEM] * 7,
+        in_specs=[VMEM] * 6,
         out_specs=pl.BlockSpec(memory_space=pltpu.HBM),
         scratch_shapes=[
             pltpu.VMEM(y.shape, F32),
-            pltpu.VMEM((STATE, rows, LANES), F32),
             pltpu.VMEM((rows, TILES * LANES), BF16),
             pltpu.SemaphoreType.DMA((4,)),
         ],
         compiler_params=params(8),
         name="finish",
-    )(got, states, sums, rate, g, y, cum)
+    )(got, states, sums, rate, y, e)
 
 
 def shards(inputs, conv_weight, conv_bias, proj_weight, dt_weight, dt_bias, decay_rate, skip_gain):
@@ -452,10 +491,10 @@
     projected = lax.all_gather(mine, "mp", axis=0, tiled=True, axis_index_groups=on_chip)
     dt, ends = state(projected, dtw, dtb, mixed, rate)
     got = lax.all_to_all(ends, "seq", 0, 0, tiled=True, axis_index_groups=on_z)
-    y, cum, rate = local(projected, dt, rate, mixed, gain)
+    y, e, rate = local(projected, dt, rate, mixed, gain)
     ends, states, sums = merge(place, got, rate, x_size)
     got = lax.all_to_all(ends, "seq", 0, 0, tiled=True, axis_index_groups=on_x)
-    return finish(got, states, sums, rate, projected, y, cum)
+    return finish(got, states, sums, rate, y, e)
 
 
 def solution(mesh):

time: 84.6 us -> 83.9 us (level)
  waiting for transfers between devices: 11.8 us -> 7.35 us
  Pallas kernels: 19.3 us -> 22.8 us
    all_to_all x1, waiting for transfers between devices: 6.55 us -> 2.05 us  [shards(): got = lax.all_to_all(ends, 'seq', 0, 0, tiled=True, axis_index_groups=on_z)]
    pallas_call x1, Pallas kernels: 5.11 us -> 9.6 us  [local(): pl.pallas_call(local_kernel, out_shape=(flat, pltpu.HBM((rows * STATE * T...]
    pallas_call x1, Pallas kernels: 4.28 us -> 3.27 us  [finish(): pl.pallas_call(finish_kernel, out_shape=jax.ShapeDtypeStruct((rows, TILES...]
  transfers between devices with their start and end apart: 2 -> 2, of which waited for: 2 -> 2; matrix products, arithmetic and copies ran while one was open for 0% -> 0% of each run, Pallas kernels for 10% -> 15%
where the time goes in v3:
time: 83.9 us; the launch traced here: 83.5 us
  blocking collectives  42.4 us (51%)
  Pallas kernels  22.8 us (27%)
  starting transfers between devices  8.78 us (10%)
  waiting for transfers between devices  7.35 us (9%)
  local copies, waits for them, and re-layouts  1.95 us (2%)
    all_to_all x1, blocking collectives, shards(): lax.all_to_all(pair(place, ours, both), 'mp', 0, 0, tiled=True, axis_inde...  17 us
    all_to_all x1, blocking collectives, shards(): lax.all_to_all(total(parts), 'mp', 0, 0, tiled=True, axis_index_groups=on_y)  11.8 us
    pallas_call x1, Pallas kernels, local(): pl.pallas_call(local_kernel, out_shape=(flat, pltpu.HBM((rows * STATE * T...  9.6 us
    all_to_all x1, blocking collectives, shards(): got = lax.all_to_all(ends, 'seq', 0, 0, tiled=True, axis_index_groups=on_x)  9.49 us
    ppermute x1, waiting for transfers between devices, shards(): lax.ppermute(inputs[rows - 8:], 'seq', [(s, s + 1) for s in range(seq - 1)])  5.3 us
    pallas_call x1, Pallas kernels, state(): pl.pallas_call(state_kernel, out_shape=(pltpu.HBM((rows * TILES, LANES),...  4.73 us
    all_to_all x1, starting transfers between devices, shards(): got = lax.all_to_all(ends, 'seq', 0, 0, tiled=True, axis_index_groups=on_z)  4.51 us
    ppermute x1, starting transfers between devices, shards(): lax.ppermute(inputs[rows - 8:], 'seq', [(s, s + 1) for s in range(seq - 1)])  4.27 us
  transfers between devices with their start and end apart: 2, of which 2 were waited for; matrix products, arithmetic and copies ran while one was open for 0% of the time, Pallas kernels for 15%

profile of v3, /device:TPU:2, one launch (start us, length us, event | category | flops | bytes accessed | tf_op | source)
XLA Modules:
  0.0 83.5 jit_solution(16240776269512722197)
XLA Ops:
  0.0 0.7 slice.3
  0.7 4.3 %collective-permute-start = (bf16[8,1024]{1,0:T(8,128)(2,1)S(1)}, bf16[8,1024]{1,0:T(8,128)(2,1)S(1)}, u32[]{:S(2)}, u32[]{:S(2)}) collective-permute-start(bf16[8,1024]{1,0:T(8,128)(2,1)S(1)} %slice.3), channel_id=1, source_target_pairs={{0,16},{16,32},{32,48},{48,64},{64,80},{80,96},{96,112},{112,128},... | collective-permute-start | bytes 49160 | tf_op jit(solution)/shard_map/ppermute | solution.py:476
  5.0 0.1 pad_add_fusion.place_ref
  5.1 2.9 %mix.1 = (bf16[256,1024]{1,0:T(8,128)(2,1)S(1)}, f32[8,1024]{1,0:T(8,128)S(1)}, bf16[256,544]{1,0:T(8,128)(2,1)S(1)}, f32[4,1024]{1,0:T(4,128)S(1)}, f32[1,1024]...) custom-call(bf16[256,1024]{1,0:T(8,128)(2,1)} %x_hbm.1, ...), custom_call_target="tpu_custom_call" | custom-call | flops 20000000 | bytes 5000000 | tf_op jit(solution)/shard_map/mix/pallas_call | solution.py:83
  8.0 5.3 %collective-permute-done.halo_ref = bf16[8,1024]{1,0:T(8,128)(2,1)S(1)} collective-permute-done((bf16[8,1024]{1,0:T(8,128)(2,1)S(1)}, bf16[8,1024]{1,0:T(8,128)(2,1)S(1)}, u32[]{:S(2)}, u32[]{:S(2)}) %collective-permute-start) | collective-permute-done | bytes 16416 | tf_op jit(solution)/shard_map/ppermute | solution.py:476
  13.3 1.0 %project.1 = (bf16[256,1024]{1,0:T(8,128)(2,1)S(1)}, bf16[128,544]{1,0:T(8,128)(2,1)S(1)}, bf16[128,544]{1,0:T(8,128)(2,1)S(1)}) custom-call(s32[3]{0:T(128)S(1)} %pad_add_fusion.place_ref, bf16[256,1024]{1,0:T(8,128)(2,1)S(1)} %get-tuple-element.26.first_ref, f32[8,1024]{1,0:T(8,128)S(1)} %get-tuple-element.27.head_ref, ...), custom_call_target="tpu_custom_call" | custom-call | tf_op jit(solution)/shard_map/project/pallas_call | solution.py:132
  14.4 2.0 %all_gather.6.got_ref = bf16[256,544]{1,0:T(8,128)(2,1)S(1)} all-gather(bf16[128,544]{1,0:T(8,128)(2,1)S(1)} %get-tuple-element.33), channel_id=1, replica_groups={{0,1},{2,3},{4,5},{6,7},{8,9},{10,11},{12,13},{14,15},{16,17},{18,19},{..., dimensions={0}, use_global_device_ids=true | all-gather | bytes 417792 | tf_op jit(solution)/shard_map/all_gather | solution.py:488
  16.4 0.6 pair.1
  17.0 17.0 %all_to_all.45 = bf16[8,16,544]{2,1,0:T(8,128)(2,1)S(1)} all-to-all(bf16[8,16,544]{2,1,0:T(8,128)(2,1)S(1)} %bitcast.20), channel_id=1, replica_groups={{0,2,4,6,8,10,12,14},{1,3,5,7,9,11,13,15},{16,18,20,22,24,26,28,30},{17..., dimensions={0} | all-to-all | bytes 278528 | tf_op jit(solution)/shard_map/all_to_all | solution.py:489
  34.0 11.8 %all_to_all.46 = bf16[8,16,544]{2,1,0:T(8,128)(2,1)S(1)} all-to-all(bf16[8,16,544]{2,1,0:T(8,128)(2,1)S(1)} %bitcast.19), channel_id=1, replica_groups={{0,2,4,6,8,10,12,14},{1,3,5,7,9,11,13,15},{16,18,20,22,24,26,28,30},{17..., dimensions={0} | all-to-all | bytes 278528 | tf_op jit(solution)/shard_map/all_to_all | solution.py:490
  45.8 2.0 %all_gather.7.g_ref = bf16[256,544]{1,0:T(8,128)(2,1)S(1)} all-gather(bf16[128,544]{1,0:T(8,128)(2,1)S(1)} %bitcast.24), channel_id=1, replica_groups={{0,1},{2,3},{4,5},{6,7},{8,9},{10,11},{12,13},{14,15},{16,17},{18,19},{..., dimensions={0}, use_global_device_ids=true | all-gather | bytes 417792 | tf_op jit(solution)/shard_map/all_gather | solution.py:491
  47.9 4.7 %state.1 = (f32[2048,128]{1,0:T(8,128)}, bf16[1152,128]{1,0:T(8,128)(2,1)}) custom-call(bf16[256,544]{1,0:T(8,128)(2,1)S(1)} %all_gather.7.g_ref, bf16[512,1024]{1,0:T(8,128)(2,1)S(1)} %get-tuple-element.34.dtw_ref, f32[1,1024]{1,0:T(1,128)S(1)} %get-tuple-element.35.dtb_ref, bf16[256,1024]{1,0:T(8,128)(2,1)S(1)} %get-tuple-element.36.mixed_ref, ...), custom_call_target="tpu_custom_call" | custom-call | tf_op jit(solution)/shard_map/state/pallas_call | solution.py:253
  52.6 4.5 %all-to-all-start.2 = ((bf16[8,144,128]{2,1,0:T(8,128)(2,1)}), bf16[8,144,128]{2,1,0:T(8,128)(2,1)S(1)}, u32[]{:S(2)}, u32[]{:S(2)}) async-start(bf16[8,144,128]{2,1,0:T(8,128)(2,1)} %bitcast.12), calls=%async_computation.2 | async-start | bytes 589824 | tf_op jit(solution)/shard_map/all_to_all | solution.py:493
  57.1 0.0 copy-start
  57.1 1.2 %copy-done = f32[2048,128]{1,0:T(8,128)S(1)} copy-done((f32[2048,128]{1,0:T(8,128)S(1)}, f32[2048,128]{1,0:T(8,128)}, u32[]{:S(2)}) %copy-start) | copy-done | bytes 1048600
  58.3 9.6 %local.1 = (f32[2048,128]{1,0:T(8,128)S(1)}, bf16[32768,128]{1,0:T(8,128)(2,1)}, f32[128,128]{1,0:T(8,128)S(1)}) custom-call(bf16[256,544]{1,0:T(8,128)(2,1)S(1)} %all_gather.7.g_ref, f32[2048,128]{1,0:T(8,128)S(1)} %copy-done, f32[128,128]{1,0:T(8,128)S(1)} %get-tuple-element.37.rate_ref, bf16[256,1024]{1,0:T(8,128)(2,1)S(1)} %get-tuple-element.36.mixed_ref, ...), custom_call_target="tpu_custom_call" | custom-call | flops 60000000 | bytes 15000000 | tf_op jit(solution)/shard_map/local/pallas_call | solution.py:333
  67.9 2.1 %all-to-all-done.2 = bf16[8,144,128]{2,1,0:T(8,128)(2,1)S(1)} async-done(((bf16[8,144,128]{2,1,0:T(8,128)(2,1)}), bf16[8,144,128]{2,1,0:T(8,128)(2,1)S(1)}, u32[]{:S(2)}, u32[]{:S(2)}) %all-to-all-start.2) | async-done | bytes 294944 | tf_op jit(solution)/shard_map/all_to_all | solution.py:493
  70.0 0.0 slice-start
  70.0 0.0 slice-start.1
  70.0 0.7 merge.1
  70.7 9.5 %all_to_all.47 = bf16[4,144,128]{2,1,0:T(8,128)(2,1)S(1)} all-to-all(bf16[4,144,128]{2,1,0:T(8,128)(2,1)S(1)} %bitcast.23), channel_id=1, replica_groups={{0,128,256,384},{16,144,272,400},{32,160,288,416},{48,176,304,432},{64,..., dimensions={0} | all-to-all | bytes 294912 | tf_op jit(solution)/shard_map/all_to_all | solution.py:496
  80.2 0.0 slice-done
  80.2 0.0 slice-done.1
  80.2 3.3 %finish.1 = bf16[256,1024]{1,0:T(8,128)(2,1)} custom-call(bf16[576,128]{1,0:T(8,128)(2,1)S(1)} %bitcast.21, f32[128,128]{1,0:T(8,128)S(1)} %get-tuple-element.43.state_ref, f32[8,128]{1,0:T(8,128)S(1)} %get-tuple-element.44.sum_ref, f32[128,128]{1,0:T(8,128)S(1)} %get-tuple-element.41.rate_ref, f32[2048,128]{1,0:T(8,128)S(1)} %get-tuple-element.45.y_ref, ...), custom_call_target="tpu_custom_call" | custom-call | tf_op jit(solution)/shard_map/finish/pallas_call | solution.py:451
  (2 shorter events, 0.0 us)
Async XLA Ops:
  0.7 12.6 %collective-permute-start = (bf16[8,1024]{1,0:T(8,128)(2,1)S(1)}, bf16[8,1024]{1,0:T(8,128)(2,1)S(1)}, u32[]{:S(2)}, u32[]{:S(2)}) collective-permute-start(bf16[8,1024]{1,0:T(8,128)(2,1)S(1)} %slice.3), channel_id=1, source_target_pairs={{0,16},{16,32},{32,48},{48,64},{64,80},{80,96},{96,112},{112,128},... | collective-permute-start | bytes 49160 | tf_op jit(solution)/shard_map/ppermute | solution.py:476
  52.6 17.4 %all-to-all-start.2 = ((bf16[8,144,128]{2,1,0:T(8,128)(2,1)}), bf16[8,144,128]{2,1,0:T(8,128)(2,1)S(1)}, u32[]{:S(2)}, u32[]{:S(2)}) async-start(bf16[8,144,128]{2,1,0:T(8,128)(2,1)} %bitcast.12), calls=%async_computation.2 | async-start | bytes 589824 | tf_op jit(solution)/shard_map/all_to_all | solution.py:493
  57.1 1.2 %copy-start = (f32[2048,128]{1,0:T(8,128)S(1)}, f32[2048,128]{1,0:T(8,128)}, u32[]{:S(2)}) copy-start(f32[2048,128]{1,0:T(8,128)} %get-tuple-element.39.dt_ref) | copy-start | bytes 3145732
  70.0 10.2 %slice-start = ((s8[8388608]{0:T(1024)(128)(4,1)}), s8[4194304]{0:T(1024)(128)(4,1)S(1)}, s32[]{:S(2)}) async-start(s8[8388608]{0:T(1024)(128)(4,1)} %bitcast.16), calls=%async_computation.4 | async-start | bytes 8388608
  70.0 10.2 %slice-start.1 = ((s8[8388608]{0:T(1024)(128)(4,1)}), s8[4194304]{0:T(1024)(128)(4,1)S(1)}, s32[]{:S(2)}) async-start(s8[8388608]{0:T(1024)(128)(4,1)} %bitcast.16), calls=%async_computation.5 | async-start | bytes 8388608

commit v4 on v3

--- a/solution.py
+++ b/solution.py
@@ -14,7 +14,6 @@
 Z = 8
 UNROLL = 16
 VMEM = pl.BlockSpec(memory_space=pltpu.VMEM)
-SMEM = pl.BlockSpec(memory_space=pltpu.SMEM)
 
 
 def params(mib):
@@ -32,13 +31,9 @@
     return pre / (1.0 + jnp.exp(-pre))
 
 
-def multiply(rows, weight_t):
-    return lax.dot_general(rows, weight_t, (((1,), (1,)), ((), ())), preferred_element_type=F32).astype(BF16)
-
-
 def mix_kernel(
     x_hbm, w_hbm, b_hbm, pw_hbm, dtw_hbm, dtb_hbm, decay_hbm, gain_hbm,
-    mixed_ref, head_ref, share_ref, w_ref, b_ref, pw_ref, dtw_ref, dtb_ref, rate_ref, gain_ref,
+    mixed_ref, head_ref, w_ref, b_ref, pw_ref, dtw_ref, dtb_ref, rate_ref, gain_ref,
     x_ref, pad_ref, decay_ref, row_ref, sems,
 ):
     rows = x_hbm.shape[0]
@@ -72,10 +67,8 @@
     for copy in later:
         copy.wait()
     for j in range(TILES):
-        c = slice(LANES * j, LANES * (j + 1))
-        rate_ref[pl.ds(j, STATE, TILES), :] = decay_ref[:, c] * -LOG2E
-        gain_ref[j : j + 1, :] = row_ref[:, c]
-    share_ref[...] = multiply(mixed_ref[...], pw_ref[...])
+        gain_ref[j : j + 1, :] = row_ref[:, lanes_of(j)]
+    rate_ref[...] = decay_ref[...] * -LOG2E
 
 
 def mix(x, weight, bias, weight_t, dtw, dtb, decay, gain):
@@ -85,17 +78,16 @@
         out_shape=(
             pltpu.VMEM((rows, width), BF16),
             pltpu.VMEM((8, width), F32),
-            pltpu.VMEM((rows, weight_t.shape[0]), BF16),
             pltpu.VMEM(weight.shape, F32),
             pltpu.VMEM(bias.shape, F32),
             pltpu.VMEM(weight_t.shape, BF16),
             pltpu.VMEM(dtw.shape, BF16),
             pltpu.VMEM(dtb.shape, F32),
-            pltpu.VMEM((STATE * TILES, LANES), F32),
+            pltpu.VMEM(decay.shape, F32),
             pltpu.VMEM((TILES, LANES), F32),
         ),
         in_specs=[pl.BlockSpec(memory_space=pltpu.HBM)] * 8,
-        out_specs=(VMEM,) * 10,
+        out_specs=(VMEM,) * 9,
         scratch_shapes=[
             pltpu.VMEM((rows, width), BF16),
             pltpu.VMEM((rows + 8, width), F32),
@@ -110,51 +102,56 @@
 
 
 def project_kernel(
-    place_ref, first_ref, head_ref, share_ref, halo_ref, w_ref, b_ref, pw_ref, mixed_ref, ours_ref, theirs_ref, pad_ref, all_ref
+    mixed_in, head_ref, halo_ref, w_ref, b_ref, pw_ref, mixed_ref, share_ref, theirs_ref, pad_ref
 ):
     pad_ref[0:8, :] = halo_ref[...].astype(F32)
     pad_ref[8:16, :] = head_ref[...]
     top = taps(pad_ref, w_ref, b_ref, 0, 8)
-    top = jnp.concatenate([top, first_ref[0:16, :].astype(F32)[8:16]], axis=0).astype(BF16)
-    mixed_ref[16:, :] = first_ref[16:, :]
-    mixed_ref[0:16, :] = top
-    all_ref[16:, :] = share_ref[16:, :]
-    all_ref[0:16, :] = multiply(top, pw_ref[...])
-    half = ours_ref.shape[0]
-    core = place_ref[2]
-    ours_ref[...] = all_ref[pl.ds(pl.multiple_of(core * half, half), half), :]
-    theirs_ref[...] = all_ref[pl.ds(pl.multiple_of((1 - core) * half, half), half), :]
-
-
-def project(place, first, head, share, halo, weight, bias, weight_t):
-    rows, width = first.shape
-    half = pltpu.VMEM((rows // 2, share.shape[1]), BF16)
+    mixed_ref[16:, :] = mixed_in[16:, :]
+    mixed_ref[0:16, :] = jnp.concatenate([top, mixed_in[0:16, :].astype(F32)[8:16]], axis=0).astype(BF16)
+    share_ref[...] = lax.dot_general(
+        mixed_ref[...], pw_ref[...], (((1,), (1,)), ((), ())), preferred_element_type=F32
+    ).astype(BF16)
+    half = theirs_ref.shape[0]
+    core = lax.rem(lax.axis_index("mp"), 2)
+    theirs_ref[...] = share_ref[pl.ds(pl.multiple_of((1 - core) * half, half), half), :]
+
+
+def project(mixed, head, halo, weight, bias, weight_t):
+    rows, width = mixed.shape
+    columns = weight_t.shape[0]
     return pl.pallas_call(
         project_kernel,
-        out_shape=(pltpu.VMEM((rows, width), BF16), half, half),
-        in_specs=[SMEM] + [VMEM] * 7,
+        out_shape=(
+            pltpu.VMEM((rows, width), BF16),
+            pltpu.VMEM((rows, columns), BF16),
+            pltpu.VMEM((rows // 2, columns), BF16),
+        ),
+        in_specs=[VMEM] * 6,
         out_specs=(VMEM,) * 3,
-        scratch_shapes=[pltpu.VMEM((16, width), F32), pltpu.VMEM(share.shape, BF16)],
+        scratch_shapes=[pltpu.VMEM((16, width), F32)],
         compiler_params=params(8),
         name="project",
-    )(place, first, head, share, halo, weight, bias, weight_t)
-
-
-def pair_kernel(place_ref, ours_ref, got_ref, out_ref):
+    )(mixed, head, halo, weight, bias, weight_t)
+
+
+def pair_kernel(share_ref, got_ref, out_ref):
     half = out_ref.shape[0]
-    theirs = pl.multiple_of((1 - place_ref[2]) * half, half)
-    out_ref[...] = (ours_ref[...].astype(F32) + got_ref[pl.ds(theirs, half), :].astype(F32)).astype(BF16)
-
-
-def pair(place, ours, got):
+    core = lax.rem(lax.axis_index("mp"), 2)
+    ours = share_ref[pl.ds(pl.multiple_of(core * half, half), half), :]
+    theirs = got_ref[pl.ds(pl.multiple_of((1 - core) * half, half), half), :]
+    out_ref[...] = (ours.astype(F32) + theirs.astype(F32)).astype(BF16)
+
+
+def pair(share, got):
     return pl.pallas_call(
         pair_kernel,
-        out_shape=jax.ShapeDtypeStruct(ours.shape, BF16),
-        in_specs=[SMEM] + [VMEM] * 2,
+        out_shape=jax.ShapeDtypeStruct((share.shape[0] // 2, share.shape[1]), BF16),
+        in_specs=[VMEM] * 2,
         out_specs=VMEM,
         compiler_params=params(8),
         name="pair",
-    )(place, ours, got)
+    )(share, got)
 
 
 def total_kernel(parts_ref, out_ref):
@@ -184,6 +181,10 @@
         )
 
 
+def lanes_of(j):
+    return slice(LANES * j, LANES * (j + 1))
+
+
 def tile(n):
     return slice(TILES * n, TILES * (n + 1))
 
@@ -192,60 +193,53 @@
     return pl.ds(pl.multiple_of(t * TILES, TILES), TILES)
 
 
-def split_sum(value):
+def send_sums(row_ref, send_ref, at, keep=None):
+    value = row_ref[...]
     high = value.astype(BF16).astype(F32)
-    return jnp.concatenate([high, value - high], axis=0)
-
-
-def sums_of(got_ref, k):
-    both = got_ref[PACK * (k + 1) - 2 * TILES : PACK * (k + 1), :].astype(F32)
-    return both[:TILES] + both[TILES:]
-
-
-def states_of(got_ref, k, n):
-    return got_ref[PACK * k + TILES * n : PACK * k + TILES * (n + 2), :].astype(F32)
+    both = jnp.concatenate([high, value - high], axis=0)
+    if keep is not None:
+        both = jnp.where(keep, both, 0.0)
+    send_ref[at : at + 2 * TILES, :] = both.astype(BF16)
 
 
 def state_kernel(
-    g_ref, dtw_ref, dtb_ref, mixed_ref, rate_ref, dt_hbm, send_ref, dt_ref, dx_ref, bc_ref, sem
+    g_ref, dtw_ref, dtb_ref, mixed_ref, rate_ref, dt_hbm, send_ref, dt_ref, enter_ref, sum_ref, sems
 ):
     rows, width = mixed_ref.shape
     low = g_ref[:, 0:DT_RANK]
-    for c in range(0, width, 256):
-        pre = jnp.dot(low, dtw_ref[:, c : c + 256], preferred_element_type=F32)
-        pre = pre + dtb_ref[:, c : c + 256]
+    enter = jnp.transpose(g_ref[:, DT_RANK : DT_RANK + 2 * STATE].astype(F32))[:STATE]
+    row = lax.broadcasted_iota(jnp.int32, enter.shape, 0)
+    for n in range(STATE):
+        enter_ref[STATE * n : STATE * (n + 1), :] = jnp.where(row == n, enter, 0.0).astype(BF16)
+    here = lax.broadcasted_iota(jnp.int32, (rows, rows), 0)
+    there = lax.broadcasted_iota(jnp.int32, (rows, rows), 1)
+    later = (there > here).astype(F32).astype(BF16)
+    copies = []
+    for i, c in enumerate(range(0, width, 256)):
+        at = slice(c, c + 256)
+        pre = jnp.dot(low, dtw_ref[:, at], preferred_element_type=F32) + dtb_ref[:, at]
         small = jnp.exp(-jnp.abs(pre))
         log1p = jnp.where(small < 1e-3, small - 0.5 * small * small, jnp.log(1.0 + small))
         dt = jnp.maximum(pre, 0.0) + log1p
-        dx = dt * mixed_ref[:, c : c + 256].astype(F32)
+        dt_ref[:, at] = dt
+        copies.append(pltpu.make_async_copy(dt_ref.at[:, at], dt_hbm.at[:, at], sems.at[i]))
+        copies[-1].start()
+        dx = dt * mixed_ref[:, at].astype(F32)
+        rem = jnp.dot(later, dt.astype(BF16), preferred_element_type=F32)
+        whole = jnp.sum(dt, axis=0, keepdims=True)
+        ends = jnp.zeros((STATE, 256), F32)
+        for n in range(STATE):
+            part = (jnp.exp2(rem * rate_ref[n : n + 1, at]) * dx).astype(BF16)
+            ends = ends + jnp.dot(enter_ref[STATE * n : STATE * (n + 1), :], part, preferred_element_type=F32)
         for h in range(2):
-            at = pl.ds(c // LANES + h, rows, TILES)
-            dt_ref[at, :] = dt[:, LANES * h : LANES * (h + 1)]
-            dx_ref[at, :] = dx[:, LANES * h : LANES * (h + 1)]
-    keep = pltpu.make_async_copy(dt_ref, dt_hbm, sem)
-    keep.start()
-    spread(g_ref[:, DT_RANK : DT_RANK + 2 * STATE].astype(F32), 0, STATE, bc_ref)
-
-    def group(i, carry):
-        states, total = list(carry[:STATE]), carry[STATE]
-        t0 = pl.multiple_of(i * UNROLL, UNROLL)
-        for r in range(UNROLL):
-            dt, dx = dt_ref[token(t0 + r), :], dx_ref[token(t0 + r), :]
-            total = total + dt
-            for n in range(STATE):
-                enter = jnp.broadcast_to(bc_ref[n, pl.ds(t0 + r, 1), :], dt.shape)
-                states[n] = jnp.exp2(dt * rate_ref[tile(n), :]) * states[n] + dx * enter
-        return (*states, total)
-
-    zero = jnp.zeros((TILES, LANES), F32)
-    final = lax.fori_loop(0, rows // UNROLL, group, (zero,) * (STATE + 1))
-    pack = [jnp.concatenate(final[n : n + 2], axis=0).astype(BF16) for n in range(0, STATE, 2)]
-    pack.append(split_sum(final[STATE]).astype(BF16))
-    for k in range(send_ref.shape[0] // PACK):
-        for i, piece in enumerate(pack):
-            at = PACK * k + 2 * TILES * i
-            send_ref[at : at + 2 * TILES, :] = piece
-    keep.wait()
+            j = c // LANES + h
+            sum_ref[j : j + 1, :] = whole[:, lanes_of(h)]
+            for k in range(Z):
+                send_ref[PACK * k + STATE * j : PACK * k + STATE * (j + 1), :] = ends[:, lanes_of(h)].astype(BF16)
+    for k in range(Z):
+        send_sums(sum_ref, send_ref, PACK * k + STATE * TILES)
+    for copy in copies:
+        copy.wait()
 
 
 def state(g, dtw, dtb, mixed, rate):
@@ -253,16 +247,16 @@
     return pl.pallas_call(
         state_kernel,
         out_shape=(
-            pltpu.HBM((rows * TILES, LANES), F32),
+            pltpu.HBM((rows, width), F32),
             pltpu.VMEM((Z * PACK, LANES), BF16),
         ),
         in_specs=[VMEM] * 5,
         out_specs=(pl.BlockSpec(memory_space=pltpu.HBM), VMEM),
         scratch_shapes=[
-            pltpu.VMEM((rows * TILES, LANES), F32),
-            pltpu.VMEM((rows * TILES, LANES), F32),
-            pltpu.VMEM((STATE, rows, LANES), F32),
-            pltpu.SemaphoreType.DMA,
+            pltpu.VMEM((rows, width), F32),
+            pltpu.VMEM((STATE * STATE, rows), BF16),
+            pltpu.VMEM((TILES, LANES), F32),
+            pltpu.SemaphoreType.DMA((width // 256,)),
         ],
         compiler_params=params(12),
         name="state",
@@ -270,14 +264,16 @@
 
 
 def local_kernel(
-    g_ref, dt_ref, rate_ref, mixed_ref, gain_ref, y_ref, e_hbm, rate_out, x_ref, bc_ref, e_ref, sems
+    g_ref, step_ref, decay_ref, mixed_ref, gain_ref, y_ref, e_hbm, rate_out, x_ref, dt_ref, rate_ref, bc_ref, e_ref, sems
 ):
     rows = mixed_ref.shape[0]
     chunk = e_ref.shape[1] // (STATE * TILES)
-    rate_out[...] = rate_ref[...]
+    rate_out[...] = decay_ref[...]
     spread(g_ref[:, DT_RANK : DT_RANK + 2 * STATE].astype(F32), 0, 2 * STATE, bc_ref)
     for j in range(TILES):
-        x_ref[pl.ds(j, rows, TILES), :] = mixed_ref[:, LANES * j : LANES * (j + 1)].astype(F32)
+        x_ref[pl.ds(j, rows, TILES), :] = mixed_ref[:, lanes_of(j)].astype(F32)
+        dt_ref[pl.ds(j, rows, TILES), :] = step_ref[:, lanes_of(j)]
+        rate_ref[pl.ds(j, STATE, TILES), :] = decay_ref[:, lanes_of(j)]
 
     def leave(i, slot):
         size = chunk * STATE * TILES
@@ -341,6 +337,8 @@
         out_specs=(VMEM, pl.BlockSpec(memory_space=pltpu.HBM), VMEM),
         scratch_shapes=[
             flat,
+            flat,
+            pltpu.VMEM((STATE * TILES, LANES), F32),
             pltpu.VMEM((2 * STATE, rows, LANES), F32),
             pltpu.VMEM((2, 32 * STATE * TILES, LANES), BF16),
             pltpu.SemaphoreType.DMA((2,)),
@@ -351,37 +349,44 @@
     )(g, dt, rate, mixed, gain)
 
 
-def merge_kernel(place_ref, got_ref, rate_ref, send_ref, state_ref, sum_ref):
+def unpack_sums(got_ref, count, sum_ref):
+    for k in range(count):
+        both = got_ref[PACK * (k + 1) - 2 * TILES : PACK * (k + 1), :].astype(F32)
+        sum_ref[TILES * k : TILES * (k + 1), :] = both[:TILES] + both[TILES:]
+
+
+def hand_on(got_ref, sum_ref, rate, k, j, run):
+    end = got_ref[PACK * k + STATE * j : PACK * k + STATE * (j + 1), :].astype(F32)
+    steps = jnp.broadcast_to(sum_ref[TILES * k + j : TILES * k + j + 1, :], end.shape)
+    return jnp.exp2(steps * rate) * run + end
+
+
+def merge_kernel(got_ref, rate_ref, send_ref, state_ref, before_ref, sum_ref, whole_ref):
     rows, count = send_ref.shape[0] // PACK, got_ref.shape[0] // PACK
-    z, x = place_ref[0], place_ref[1]
-    zero = jnp.zeros((TILES, LANES), F32)
-    sums = [sums_of(got_ref, k) for k in range(count)]
-    whole, before = zero, zero
+    me = lax.axis_index("seq")
+    z, x = lax.rem(me, Z), me // Z
+    unpack_sums(got_ref, count, sum_ref)
+    whole = before = jnp.zeros((TILES, LANES), F32)
     for k in range(count):
-        whole = whole + sums[k]
-        before = before + jnp.where(k < z, sums[k], 0.0)
-    sum_ref[...] = before
-    for n in range(0, STATE, 2):
-        blocks = [states_of(got_ref, k, n) for k in range(count)]
-        ends, held = [], []
-        for h in range(2):
-            run, keep = zero, zero
-            for k in range(count):
-                keep = jnp.where(k == z, run, keep)
-                run = jnp.exp2(sums[k] * rate_ref[tile(n + h), :]) * run + blocks[k][tile(h)]
-            ends.append(run)
-            held.append(keep)
-        state_ref[TILES * n : TILES * (n + 2), :] = jnp.concatenate(held, axis=0)
-        both = jnp.concatenate(ends, axis=0)
+        steps = sum_ref[TILES * k : TILES * (k + 1), :]
+        whole = whole + steps
+        before = before + jnp.where(k < z, steps, 0.0)
+    before_ref[...] = before
+    whole_ref[...] = whole
+    for j in range(TILES):
+        rate = rate_ref[:, lanes_of(j)]
+        run = kept = jnp.zeros((STATE, LANES), F32)
+        for k in range(count):
+            kept = jnp.where(k == z, run, kept)
+            run = hand_on(got_ref, sum_ref, rate, k, j, run)
+        state_ref[STATE * j : STATE * (j + 1), :] = kept
         for d in range(rows):
-            at = PACK * d + TILES * n
-            send_ref[at : at + 2 * TILES, :] = jnp.where(d > x, both, 0.0).astype(BF16)
-    both = split_sum(whole)
+            send_ref[PACK * d + STATE * j : PACK * d + STATE * (j + 1), :] = jnp.where(d > x, run, 0.0).astype(BF16)
     for d in range(rows):
-        send_ref[PACK * (d + 1) - 2 * TILES : PACK * (d + 1), :] = jnp.where(d > x, both, 0.0).astype(BF16)
-
-
-def merge(place, got, rate, rows):
+        send_sums(whole_ref, send_ref, PACK * d + STATE * TILES, d > x)
+
+
+def merge(got, rate, rows):
     return pl.pallas_call(
         merge_kernel,
         out_shape=(
@@ -389,27 +394,30 @@
             pltpu.VMEM((STATE * TILES, LANES), F32),
             pltpu.VMEM((TILES, LANES), F32),
         ),
-        in_specs=[SMEM, VMEM, VMEM],
+        in_specs=[VMEM, VMEM],
         out_specs=(VMEM,) * 3,
+        scratch_shapes=[pltpu.VMEM((Z * TILES, LANES), F32), pltpu.VMEM((TILES, LANES), F32)],
         compiler_params=params(8),
         cost_estimate=cost(100_000_000),
         name="merge",
-    )(place, got, rate)
-
-
-def finish_kernel(got_ref, state_ref, sum_ref, rate_ref, y_ref, e_ref, out_hbm, tot_ref, out_ref, sems):
+    )(got, rate)
+
+
+def finish_kernel(
+    got_ref, state_ref, before_ref, rate_ref, y_ref, e_ref, out_hbm, tot_ref, out_ref, sum_ref, in_ref, sems
+):
     rows = out_hbm.shape[0]
     count = got_ref.shape[0] // PACK - 1
-    sums = [sums_of(got_ref, k) for k in range(count)]
-    incoming = []
-    for n in range(0, STATE, 2):
-        blocks = [states_of(got_ref, k, n) for k in range(count)]
-        for h in range(2):
-            rate = rate_ref[tile(n + h), :]
-            run = blocks[0][tile(h)]
-            for k in range(1, count):
-                run = jnp.exp2(sums[k] * rate) * run + blocks[k][tile(h)]
-            incoming.append(jnp.exp2(sum_ref[...] * rate) * run + state_ref[tile(n + h), :])
+    unpack_sums(got_ref, count, sum_ref)
+    for j in range(TILES):
+        rate = rate_ref[:, lanes_of(j)]
+        run = jnp.zeros((STATE, LANES), F32)
+        for k in range(count):
+            run = hand_on(got_ref, sum_ref, rate, k, j, run)
+        steps = jnp.broadcast_to(before_ref[j : j + 1, :], run.shape)
+        at = slice(STATE * j, STATE * (j + 1))
+        in_ref[at, :] = jnp.exp2(steps * rate) * run + state_ref[at, :]
+    incoming = [in_ref[pl.ds(n, TILES, STATE), :] for n in range(STATE)]
 
     def group(i, carry):
         t0 = pl.multiple_of(i * UNROLL, UNROLL)
@@ -456,6 +464,8 @@
         scratch_shapes=[
             pltpu.VMEM(y.shape, F32),
             pltpu.VMEM((rows, TILES * LANES), BF16),
+            pltpu.VMEM((Z * TILES, LANES), F32),
+            pltpu.VMEM((STATE * TILES, LANES), F32),
             pltpu.SemaphoreType.DMA((4,)),
         ],
         compiler_params=params(8),
@@ -471,10 +481,9 @@
     on_x = [[Z * x + z for x in range(x_size)] for z in range(Z)]
     on_y = [[2 * y + core for y in range(y_size)] for core in range(2)]
     on_chip = [[2 * y, 2 * y + 1] for y in range(y_size)]
-    me = lax.axis_index("seq")
-    place = jnp.stack([me % Z, me // Z, lax.axis_index("mp") % 2]).astype(jnp.int32)
+
     halo = lax.ppermute(inputs[rows - 8 :], "seq", [(s, s + 1) for s in range(seq - 1)])
-    first, head, share, taps_in, bias, weight, dtw, dtb, rate, gain = mix(
+    mixed, head, taps_in, bias, weight, dtw, dtb, rate, gain = mix(
         inputs,
         conv_weight,
         conv_bias.reshape(1, width),
@@ -484,15 +493,15 @@
         jnp.transpose(decay_rate),
         skip_gain.reshape(1, width),
     )
-    mixed, ours, theirs = project(place, first, head, share, halo, taps_in, bias, weight)
+    mixed, share, theirs = project(mixed, head, halo, taps_in, bias, weight)
     both = lax.all_gather(theirs, "mp", axis=0, tiled=True, axis_index_groups=on_chip)
-    parts = lax.all_to_all(pair(place, ours, both), "mp", 0, 0, tiled=True, axis_index_groups=on_y)
+    parts = lax.all_to_all(pair(share, both), "mp", 0, 0, tiled=True, axis_index_groups=on_y)
     mine = lax.all_to_all(total(parts), "mp", 0, 0, tiled=True, axis_index_groups=on_y)
     projected = lax.all_gather(mine, "mp", axis=0, tiled=True, axis_index_groups=on_chip)
     dt, ends = state(projected, dtw, dtb, mixed, rate)
     got = lax.all_to_all(ends, "seq", 0, 0, tiled=True, axis_index_groups=on_z)
     y, e, rate = local(projected, dt, rate, mixed, gain)
-    ends, states, sums = merge(place, got, rate, x_size)
+    ends, states, sums = merge(got, rate, x_size)
     got = lax.all_to_all(ends, "seq", 0, 0, tiled=True, axis_index_groups=on_x)
     return finish(got, states, sums, rate, y, e)
 

time: 83.9 us -> 82.3 us (0.981)
  Pallas kernels: 22.8 us -> 20.8 us
where the time goes in v4:
time: 82.3 us; the launch traced here: 81.8 us
  blocking collectives  42.4 us (52%)
  Pallas kernels  20.8 us (25%)
  starting transfers between devices  8.76 us (11%)
  waiting for transfers between devices  7.89 us (10%)
  local copies, waits for them, and re-layouts  1.95 us (2%)
    all_to_all x1, blocking collectives, shards(): lax.all_to_all(pair(share, both), 'mp', 0, 0, tiled=True, axis_index_grou...  17 us
    all_to_all x1, blocking collectives, shards(): lax.all_to_all(total(parts), 'mp', 0, 0, tiled=True, axis_index_groups=on_y)  11.8 us
    pallas_call x1, Pallas kernels, local(): pl.pallas_call(local_kernel, out_shape=(flat, pltpu.HBM((rows * STATE * T...  9.79 us
    all_to_all x1, blocking collectives, shards(): got = lax.all_to_all(ends, 'seq', 0, 0, tiled=True, axis_index_groups=on_x)  9.5 us
    ppermute x1, waiting for transfers between devices, shards(): lax.ppermute(inputs[rows - 8:], 'seq', [(s, s + 1) for s in range(seq - 1)])  6.02 us
    pallas_call x1, Pallas kernels, state(): pl.pallas_call(state_kernel, out_shape=(pltpu.HBM((rows, width), F32), pl...  4.53 us
    all_to_all x1, starting transfers between devices, shards(): got = lax.all_to_all(ends, 'seq', 0, 0, tiled=True, axis_index_groups=on_z)  4.49 us
    ppermute x1, starting transfers between devices, shards(): lax.ppermute(inputs[rows - 8:], 'seq', [(s, s + 1) for s in range(seq - 1)])  4.27 us
  transfers between devices with their start and end apart: 2, of which 2 were waited for; matrix products, arithmetic and copies ran while one was open for 0% of the time, Pallas kernels for 15%

profile of v4, /device:TPU:2, one launch (start us, length us, event | category | flops | bytes accessed | tf_op | source)
XLA Modules:
  0.0 81.8 jit_solution(16972665020645538907)
XLA Ops:
  0.0 0.7 slice.3
  0.7 4.3 %collective-permute-start = (bf16[8,1024]{1,0:T(8,128)(2,1)S(1)}, bf16[8,1024]{1,0:T(8,128)(2,1)S(1)}, u32[]{:S(2)}, u32[]{:S(2)}) collective-permute-start(bf16[8,1024]{1,0:T(8,128)(2,1)S(1)} %slice.3), channel_id=1, source_target_pairs={{0,16},{16,32},{32,48},{48,64},{64,80},{80,96},{96,112},{112,128},... | collective-permute-start | bytes 49160 | tf_op jit(solution)/shard_map/ppermute | solution.py:485
  5.0 2.3 %mix.1 = (bf16[256,1024]{1,0:T(8,128)(2,1)S(1)}, f32[8,1024]{1,0:T(8,128)S(1)}, f32[4,1024]{1,0:T(4,128)S(1)}, f32[1,1024]{1,0:T(1,128)S(1)}, bf16[544,1024]{1,0...) custom-call(bf16[256,1024]{1,0:T(8,128)(2,1)} %x_hbm.1, ...), custom_call_target="tpu_custom_call" | custom-call | flops 20000000 | bytes 5000000 | tf_op jit(solution)/shard_map/mix/pallas_call | solution.py:76
  7.3 6.0 %collective-permute-done.halo_ref = bf16[8,1024]{1,0:T(8,128)(2,1)S(1)} collective-permute-done((bf16[8,1024]{1,0:T(8,128)(2,1)S(1)}, bf16[8,1024]{1,0:T(8,128)(2,1)S(1)}, u32[]{:S(2)}, u32[]{:S(2)}) %collective-permute-start) | collective-permute-done | bytes 16416 | tf_op jit(solution)/shard_map/ppermute | solution.py:485
  13.3 0.7 project.1
  14.0 2.0 %all_gather.6.got_ref = bf16[256,544]{1,0:T(8,128)(2,1)S(1)} all-gather(bf16[128,544]{1,0:T(8,128)(2,1)S(1)} %get-tuple-element.31), channel_id=1, replica_groups={{0,1},{2,3},{4,5},{6,7},{8,9},{10,11},{12,13},{14,15},{16,17},{18,19},{..., dimensions={0}, use_global_device_ids=true | all-gather | bytes 417792 | tf_op jit(solution)/shard_map/all_gather | solution.py:497
  16.1 17.0 %all_to_all.45 = bf16[8,16,544]{2,1,0:T(8,128)(2,1)S(1)} all-to-all(bf16[8,16,544]{2,1,0:T(8,128)(2,1)S(1)} %bitcast.17), channel_id=1, replica_groups={{0,2,4,6,8,10,12,14},{1,3,5,7,9,11,13,15},{16,18,20,22,24,26,28,30},{17..., dimensions={0} | all-to-all | bytes 278528 | tf_op jit(solution)/shard_map/all_to_all | solution.py:498
  33.1 11.8 %all_to_all.46 = bf16[8,16,544]{2,1,0:T(8,128)(2,1)S(1)} all-to-all(bf16[8,16,544]{2,1,0:T(8,128)(2,1)S(1)} %bitcast.16), channel_id=1, replica_groups={{0,2,4,6,8,10,12,14},{1,3,5,7,9,11,13,15},{16,18,20,22,24,26,28,30},{17..., dimensions={0} | all-to-all | bytes 278528 | tf_op jit(solution)/shard_map/all_to_all | solution.py:499
  44.9 2.0 %all_gather.7.g_ref = bf16[256,544]{1,0:T(8,128)(2,1)S(1)} all-gather(bf16[128,544]{1,0:T(8,128)(2,1)S(1)} %bitcast.21), channel_id=1, replica_groups={{0,1},{2,3},{4,5},{6,7},{8,9},{10,11},{12,13},{14,15},{16,17},{18,19},{..., dimensions={0}, use_global_device_ids=true | all-gather | bytes 417792 | tf_op jit(solution)/shard_map/all_gather | solution.py:500
  47.0 4.5 %state.1 = (f32[256,1024]{1,0:T(8,128)}, bf16[1152,128]{1,0:T(8,128)(2,1)}) custom-call(bf16[256,544]{1,0:T(8,128)(2,1)S(1)} %all_gather.7.g_ref, bf16[512,1024]{1,0:T(8,128)(2,1)S(1)} %get-tuple-element.32.dtw_ref, f32[1,1024]{1,0:T(1,128)S(1)} %get-tuple-element.33.dtb_ref, bf16[256,1024]{1,0:T(8,128)(2,1)S(1)} %get-tuple-element.34.mixed_ref, ...), custom_call_target="tpu_custom_call" | custom-call | tf_op jit(solution)/shard_map/state/pallas_call | solution.py:247
  51.5 4.5 %all-to-all-start.2 = ((bf16[8,144,128]{2,1,0:T(8,128)(2,1)}), bf16[8,144,128]{2,1,0:T(8,128)(2,1)S(1)}, u32[]{:S(2)}, u32[]{:S(2)}) async-start(bf16[8,144,128]{2,1,0:T(8,128)(2,1)} %bitcast.9), calls=%async_computation.2 | async-start | bytes 589824 | tf_op jit(solution)/shard_map/all_to_all | solution.py:502
  56.0 0.0 copy-start
  56.0 1.2 %copy-done = f32[256,1024]{1,0:T(8,128)S(1)} copy-done((f32[256,1024]{1,0:T(8,128)S(1)}, f32[256,1024]{1,0:T(8,128)}, u32[]{:S(2)}) %copy-start) | copy-done | bytes 1048600
  57.2 9.8 %local.1 = (f32[2048,128]{1,0:T(8,128)S(1)}, bf16[32768,128]{1,0:T(8,128)(2,1)}, f32[16,1024]{1,0:T(8,128)S(1)}) custom-call(bf16[256,544]{1,0:T(8,128)(2,1)S(1)} %all_gather.7.g_ref, f32[256,1024]{1,0:T(8,128)S(1)} %copy-done, f32[16,1024]{1,0:T(8,128)S(1)} %get-tuple-element.35.rate_ref.decay_ref, bf16[256,1024]{1,0:T(8,128)(2,1)S(1)} %get-tuple-element.34.mixed_ref, ...), custom_call_target="tpu_custom_call" | custom-call | flops 60000000 | bytes 15000000 | tf_op jit(solution)/shard_map/local/pallas_call | solution.py:329
  67.0 1.9 %all-to-all-done.2 = bf16[8,144,128]{2,1,0:T(8,128)(2,1)S(1)} async-done(((bf16[8,144,128]{2,1,0:T(8,128)(2,1)}), bf16[8,144,128]{2,1,0:T(8,128)(2,1)S(1)}, u32[]{:S(2)}, u32[]{:S(2)}) %all-to-all-start.2) | async-done | bytes 294944 | tf_op jit(solution)/shard_map/all_to_all | solution.py:502
  68.9 0.0 slice-start
  68.9 0.0 slice-start.1
  68.9 0.1 merge.1
  69.0 9.5 %all_to_all.47 = bf16[4,144,128]{2,1,0:T(8,128)(2,1)S(1)} all-to-all(bf16[4,144,128]{2,1,0:T(8,128)(2,1)S(1)} %bitcast.20), channel_id=1, replica_groups={{0,128,256,384},{16,144,272,400},{32,160,288,416},{48,176,304,432},{64,..., dimensions={0} | all-to-all | bytes 294912 | tf_op jit(solution)/shard_map/all_to_all | solution.py:505
  78.5 0.0 slice-done
  78.5 0.0 slice-done.1
  78.5 3.3 %finish.1 = bf16[256,1024]{1,0:T(8,128)(2,1)} custom-call(bf16[576,128]{1,0:T(8,128)(2,1)S(1)} %bitcast.18, f32[128,128]{1,0:T(8,128)S(1)} %get-tuple-element.41.state_ref, f32[8,128]{1,0:T(8,128)S(1)} %get-tuple-element.42.before_ref, f32[16,1024]{1,0:T(8,128)S(1)} %get-tuple-element.39.rate_ref, f32[2048,128]{1,0:T(8,128)S(1)} %get-tuple-element.43.y_ref, ...), custom_call_target="tpu_custom_call" | custom-call | tf_op jit(solution)/shard_map/finish/pallas_call | solution.py:459
  (3 shorter events, 0.1 us)
Async XLA Ops:
  0.7 12.6 %collective-permute-start = (bf16[8,1024]{1,0:T(8,128)(2,1)S(1)}, bf16[8,1024]{1,0:T(8,128)(2,1)S(1)}, u32[]{:S(2)}, u32[]{:S(2)}) collective-permute-start(bf16[8,1024]{1,0:T(8,128)(2,1)S(1)} %slice.3), channel_id=1, source_target_pairs={{0,16},{16,32},{32,48},{48,64},{64,80},{80,96},{96,112},{112,128},... | collective-permute-start | bytes 49160 | tf_op jit(solution)/shard_map/ppermute | solution.py:485
  51.5 17.4 %all-to-all-start.2 = ((bf16[8,144,128]{2,1,0:T(8,128)(2,1)}), bf16[8,144,128]{2,1,0:T(8,128)(2,1)S(1)}, u32[]{:S(2)}, u32[]{:S(2)}) async-start(bf16[8,144,128]{2,1,0:T(8,128)(2,1)} %bitcast.9), calls=%async_computation.2 | async-start | bytes 589824 | tf_op jit(solution)/shard_map/all_to_all | solution.py:502
  56.0 1.2 %copy-start = (f32[256,1024]{1,0:T(8,128)S(1)}, f32[256,1024]{1,0:T(8,128)}, u32[]{:S(2)}) copy-start(f32[256,1024]{1,0:T(8,128)} %get-tuple-element.37.step_ref) | copy-start | bytes 3145732
  68.9 9.6 %slice-start = ((s8[8388608]{0:T(1024)(128)(4,1)}), s8[4194304]{0:T(1024)(128)(4,1)S(1)}, s32[]{:S(2)}) async-start(s8[8388608]{0:T(1024)(128)(4,1)} %bitcast.13), calls=%async_computation.4 | async-start | bytes 8388608
  68.9 9.6 %slice-start.1 = ((s8[8388608]{0:T(1024)(128)(4,1)}), s8[4194304]{0:T(1024)(128)(4,1)S(1)}, s32[]{:S(2)}) async-start(s8[8388608]{0:T(1024)(128)(4,1)} %bitcast.13), calls=%async_computation.5 | async-start | bytes 8388608

commit v5 on v4

--- a/solution.py
+++ b/solution.py
@@ -289,17 +289,12 @@
                 dt, x = dt_ref[token(t), :], x_ref[token(t), :]
                 dx, y = dt * x, gain_ref[...] * x
                 total = total + dt
-                weights = []
                 for n in range(STATE):
                     enter = jnp.broadcast_to(bc_ref[n, pl.ds(t, 1), :], dt.shape)
                     read = jnp.broadcast_to(bc_ref[STATE + n, pl.ds(t, 1), :], dt.shape)
                     states[n] = jnp.exp2(dt * rate_ref[tile(n), :]) * states[n] + dx * enter
                     y = y + states[n] * read
-                    weights.append(jnp.exp2(total * rate_ref[tile(n), :]) * read)
-                    if n % 2:
-                        at = (t0 + r) * (STATE * TILES) + TILES * (n - 1)
-                        both = jnp.concatenate(weights[n - 1 :], axis=0).astype(BF16)
-                        e_ref[slot, pl.ds(pl.multiple_of(at, 2 * TILES), 2 * TILES), :] = both
+                    e_ref[slot, token((t0 + r) * STATE + n), :] = jnp.exp2(total * rate_ref[tile(n), :]) * read
                 y_ref[token(t), :] = y
             return (*states, total)
 
@@ -330,7 +325,7 @@
         local_kernel,
         out_shape=(
             flat,
-            pltpu.HBM((rows * STATE * TILES, LANES), BF16),
+            pltpu.HBM((rows * STATE * TILES, LANES), F32),
             pltpu.VMEM(rate.shape, F32),
         ),
         in_specs=[VMEM] * 5,
@@ -340,7 +335,7 @@
             flat,
             pltpu.VMEM((STATE * TILES, LANES), F32),
             pltpu.VMEM((2 * STATE, rows, LANES), F32),
-            pltpu.VMEM((2, 32 * STATE * TILES, LANES), BF16),
+            pltpu.VMEM((2, 32 * STATE * TILES, LANES), F32),
             pltpu.SemaphoreType.DMA((2,)),
         ],
         compiler_params=params(12),
@@ -398,7 +393,7 @@
         out_specs=(VMEM,) * 3,
         scratch_shapes=[pltpu.VMEM((Z * TILES, LANES), F32), pltpu.VMEM((TILES, LANES), F32)],
         compiler_params=params(8),
-        cost_estimate=cost(100_000_000),
+        cost_estimate=cost(200_000_000),
         name="merge",
     )(got, rate)
 
@@ -423,11 +418,7 @@
         t0 = pl.multiple_of(i * UNROLL, UNROLL)
         for r in range(UNROLL):
             t = t0 + r
-            more = []
-            for n in range(0, STATE, 2):
-                at = pl.multiple_of(t * STATE * TILES + n * TILES, 2 * TILES)
-                both = e_ref[pl.ds(at, 2 * TILES), :].astype(F32)
-                more.append(both[:TILES] * carry[n] + both[TILES:] * carry[n + 1])
+            more = [e_ref[token(t * STATE + n), :] * carry[n] for n in range(STATE)]
             while len(more) > 1:
                 more = [a + b for a, b in zip(more[::2], more[1::2])]
             tot_ref[token(t), :] = y_ref[token(t), :] + more[0]

time: 82.3 us -> 81.2 us (0.987)
    pallas_call x1, Pallas kernels: 3.3 us -> 2.17 us  [finish(): pl.pallas_call(finish_kernel, out_shape=jax.ShapeDtypeStruct((rows, TILES...]
where the time goes in v5:
time: 81.2 us; the launch traced here: 80.7 us
  blocking collectives  42.4 us (52%)
  Pallas kernels  20.1 us (25%)
  starting transfers between devices  8.76 us (11%)
  waiting for transfers between devices  7.5 us (9%)
  local copies, waits for them, and re-layouts  1.95 us (2%)
    all_to_all x1, blocking collectives, shards(): lax.all_to_all(pair(share, both), 'mp', 0, 0, tiled=True, axis_index_grou...  17 us
    all_to_all x1, blocking collectives, shards(): lax.all_to_all(total(parts), 'mp', 0, 0, tiled=True, axis_index_groups=on_y)  11.8 us
    pallas_call x1, Pallas kernels, local(): pl.pallas_call(local_kernel, out_shape=(flat, pltpu.HBM((rows * STATE * T...  10.2 us
    all_to_all x1, blocking collectives, shards(): got = lax.all_to_all(ends, 'seq', 0, 0, tiled=True, axis_index_groups=on_x)  9.5 us
    ppermute x1, waiting for transfers between devices, shards(): lax.ppermute(inputs[rows - 8:], 'seq', [(s, s + 1) for s in range(seq - 1)])  6.02 us
    pallas_call x1, Pallas kernels, state(): pl.pallas_call(state_kernel, out_shape=(pltpu.HBM((rows, width), F32), pl...  4.53 us
    all_to_all x1, starting transfers between devices, shards(): got = lax.all_to_all(ends, 'seq', 0, 0, tiled=True, axis_index_groups=on_z)  4.49 us
    ppermute x1, starting transfers between devices, shards(): lax.ppermute(inputs[rows - 8:], 'seq', [(s, s + 1) for s in range(seq - 1)])  4.27 us
  transfers between devices with their start and end apart: 2, of which 2 were waited for; matrix products, arithmetic and copies ran while one was open for 0% of the time, Pallas kernels for 15%

profile of v5, /device:TPU:2, one launch (start us, length us, event | category | flops | bytes accessed | tf_op | source)
XLA Modules:
  0.0 80.7 jit_solution(679667180896659712)
XLA Ops:
  0.0 0.7 slice.3
  0.7 4.3 %collective-permute-start = (bf16[8,1024]{1,0:T(8,128)(2,1)S(1)}, bf16[8,1024]{1,0:T(8,128)(2,1)S(1)}, u32[]{:S(2)}, u32[]{:S(2)}) collective-permute-start(bf16[8,1024]{1,0:T(8,128)(2,1)S(1)} %slice.3), channel_id=1, source_target_pairs={{0,16},{16,32},{32,48},{48,64},{64,80},{80,96},{96,112},{112,128},... | collective-permute-start | bytes 49160 | tf_op jit(solution)/shard_map/ppermute | solution.py:476
  5.0 2.3 %mix.1 = (bf16[256,1024]{1,0:T(8,128)(2,1)S(1)}, f32[8,1024]{1,0:T(8,128)S(1)}, f32[4,1024]{1,0:T(4,128)S(1)}, f32[1,1024]{1,0:T(1,128)S(1)}, bf16[544,1024]{1,0...) custom-call(bf16[256,1024]{1,0:T(8,128)(2,1)} %x_hbm.1, ...), custom_call_target="tpu_custom_call" | custom-call | flops 20000000 | bytes 5000000 | tf_op jit(solution)/shard_map/mix/pallas_call | solution.py:76
  7.3 6.0 %collective-permute-done.halo_ref = bf16[8,1024]{1,0:T(8,128)(2,1)S(1)} collective-permute-done((bf16[8,1024]{1,0:T(8,128)(2,1)S(1)}, bf16[8,1024]{1,0:T(8,128)(2,1)S(1)}, u32[]{:S(2)}, u32[]{:S(2)}) %collective-permute-start) | collective-permute-done | bytes 16416 | tf_op jit(solution)/shard_map/ppermute | solution.py:476
  13.3 0.7 project.1
  14.0 2.0 %all_gather.6.got_ref = bf16[256,544]{1,0:T(8,128)(2,1)S(1)} all-gather(bf16[128,544]{1,0:T(8,128)(2,1)S(1)} %get-tuple-element.31), channel_id=1, replica_groups={{0,1},{2,3},{4,5},{6,7},{8,9},{10,11},{12,13},{14,15},{16,17},{18,19},{..., dimensions={0}, use_global_device_ids=true | all-gather | bytes 417792 | tf_op jit(solution)/shard_map/all_gather | solution.py:488
  16.1 17.0 %all_to_all.45 = bf16[8,16,544]{2,1,0:T(8,128)(2,1)S(1)} all-to-all(bf16[8,16,544]{2,1,0:T(8,128)(2,1)S(1)} %bitcast.17), channel_id=1, replica_groups={{0,2,4,6,8,10,12,14},{1,3,5,7,9,11,13,15},{16,18,20,22,24,26,28,30},{17..., dimensions={0} | all-to-all | bytes 278528 | tf_op jit(solution)/shard_map/all_to_all | solution.py:489
  33.1 11.8 %all_to_all.46 = bf16[8,16,544]{2,1,0:T(8,128)(2,1)S(1)} all-to-all(bf16[8,16,544]{2,1,0:T(8,128)(2,1)S(1)} %bitcast.16), channel_id=1, replica_groups={{0,2,4,6,8,10,12,14},{1,3,5,7,9,11,13,15},{16,18,20,22,24,26,28,30},{17..., dimensions={0} | all-to-all | bytes 278528 | tf_op jit(solution)/shard_map/all_to_all | solution.py:490
  44.9 2.0 %all_gather.7.g_ref = bf16[256,544]{1,0:T(8,128)(2,1)S(1)} all-gather(bf16[128,544]{1,0:T(8,128)(2,1)S(1)} %bitcast.21), channel_id=1, replica_groups={{0,1},{2,3},{4,5},{6,7},{8,9},{10,11},{12,13},{14,15},{16,17},{18,19},{..., dimensions={0}, use_global_device_ids=true | all-gather | bytes 417792 | tf_op jit(solution)/shard_map/all_gather | solution.py:491
  47.0 4.5 %state.1 = (f32[256,1024]{1,0:T(8,128)}, bf16[1152,128]{1,0:T(8,128)(2,1)}) custom-call(bf16[256,544]{1,0:T(8,128)(2,1)S(1)} %all_gather.7.g_ref, bf16[512,1024]{1,0:T(8,128)(2,1)S(1)} %get-tuple-element.32.dtw_ref, f32[1,1024]{1,0:T(1,128)S(1)} %get-tuple-element.33.dtb_ref, bf16[256,1024]{1,0:T(8,128)(2,1)S(1)} %get-tuple-element.34.mixed_ref, ...), custom_call_target="tpu_custom_call" | custom-call | tf_op jit(solution)/shard_map/state/pallas_call | solution.py:247
  51.5 4.5 %all-to-all-start.2 = ((bf16[8,144,128]{2,1,0:T(8,128)(2,1)}), bf16[8,144,128]{2,1,0:T(8,128)(2,1)S(1)}, u32[]{:S(2)}, u32[]{:S(2)}) async-start(bf16[8,144,128]{2,1,0:T(8,128)(2,1)} %bitcast.9), calls=%async_computation.2 | async-start | bytes 589824 | tf_op jit(solution)/shard_map/all_to_all | solution.py:493
  56.0 0.0 copy-start
  56.0 1.2 %copy-done = f32[256,1024]{1,0:T(8,128)S(1)} copy-done((f32[256,1024]{1,0:T(8,128)S(1)}, f32[256,1024]{1,0:T(8,128)}, u32[]{:S(2)}) %copy-start) | copy-done | bytes 1048600
  57.2 10.2 %local.1 = (f32[2048,128]{1,0:T(8,128)S(1)}, f32[32768,128]{1,0:T(8,128)}, f32[16,1024]{1,0:T(8,128)S(1)}) custom-call(bf16[256,544]{1,0:T(8,128)(2,1)S(1)} %all_gather.7.g_ref, f32[256,1024]{1,0:T(8,128)S(1)} %copy-done, f32[16,1024]{1,0:T(8,128)S(1)} %get-tuple-element.35.rate_ref.decay_ref, bf16[256,1024]{1,0:T(8,128)(2,1)S(1)} %get-tuple-element.34.mixed_ref, ...), custom_call_target="tpu_custom_call" | custom-call | flops 60000000 | bytes 15000000 | tf_op jit(solution)/shard_map/local/pallas_call | solution.py:324
  67.4 1.5 %all-to-all-done.2 = bf16[8,144,128]{2,1,0:T(8,128)(2,1)S(1)} async-done(((bf16[8,144,128]{2,1,0:T(8,128)(2,1)}), bf16[8,144,128]{2,1,0:T(8,128)(2,1)S(1)}, u32[]{:S(2)}, u32[]{:S(2)}) %all-to-all-start.2) | async-done | bytes 294944 | tf_op jit(solution)/shard_map/all_to_all | solution.py:493
  68.9 0.0 slice-start
  68.9 0.0 slice-start.1
  68.9 0.0 slice-start.2
  68.9 0.0 slice-start.3
  68.9 0.1 merge.1
  69.0 9.5 %all_to_all.47 = bf16[4,144,128]{2,1,0:T(8,128)(2,1)S(1)} all-to-all(bf16[4,144,128]{2,1,0:T(8,128)(2,1)S(1)} %bitcast.20), channel_id=1, replica_groups={{0,128,256,384},{16,144,272,400},{32,160,288,416},{48,176,304,432},{64,..., dimensions={0} | all-to-all | bytes 294912 | tf_op jit(solution)/shard_map/all_to_all | solution.py:496
  78.5 0.0 slice-done
  78.5 0.0 slice-done.1
  78.5 0.0 slice-done.2
  78.5 0.0 slice-done.3
  78.5 2.2 %finish.1 = bf16[256,1024]{1,0:T(8,128)(2,1)} custom-call(bf16[576,128]{1,0:T(8,128)(2,1)S(1)} %bitcast.18, f32[128,128]{1,0:T(8,128)S(1)} %get-tuple-element.41.state_ref, f32[8,128]{1,0:T(8,128)S(1)} %get-tuple-element.42.before_ref, f32[16,1024]{1,0:T(8,128)S(1)} %get-tuple-element.39.rate_ref, f32[2048,128]{1,0:T(8,128)S(1)} %get-tuple-element.43.y_ref, ...), custom_call_target="tpu_custom_call" | custom-call | tf_op jit(solution)/shard_map/finish/pallas_call | solution.py:450
  (3 shorter events, 0.1 us)
Async XLA Ops:
  0.7 12.6 %collective-permute-start = (bf16[8,1024]{1,0:T(8,128)(2,1)S(1)}, bf16[8,1024]{1,0:T(8,128)(2,1)S(1)}, u32[]{:S(2)}, u32[]{:S(2)}) collective-permute-start(bf16[8,1024]{1,0:T(8,128)(2,1)S(1)} %slice.3), channel_id=1, source_target_pairs={{0,16},{16,32},{32,48},{48,64},{64,80},{80,96},{96,112},{112,128},... | collective-permute-start | bytes 49160 | tf_op jit(solution)/shard_map/ppermute | solution.py:476
  51.5 17.4 %all-to-all-start.2 = ((bf16[8,144,128]{2,1,0:T(8,128)(2,1)}), bf16[8,144,128]{2,1,0:T(8,128)(2,1)S(1)}, u32[]{:S(2)}, u32[]{:S(2)}) async-start(bf16[8,144,128]{2,1,0:T(8,128)(2,1)} %bitcast.9), calls=%async_computation.2 | async-start | bytes 589824 | tf_op jit(solution)/shard_map/all_to_all | solution.py:493
  56.0 1.2 %copy-start = (f32[256,1024]{1,0:T(8,128)S(1)}, f32[256,1024]{1,0:T(8,128)}, u32[]{:S(2)}) copy-start(f32[256,1024]{1,0:T(8,128)} %get-tuple-element.37.step_ref) | copy-start | bytes 3145732
  68.9 9.7 %slice-start = ((s8[16777216]{0:T(1024)(128)(4,1)}), s8[4194304]{0:T(1024)(128)(4,1)S(1)}, s32[]{:S(2)}) async-start(s8[16777216]{0:T(1024)(128)(4,1)} %bitcast.13), calls=%async_computation.4 | async-start | bytes 8388608
  68.9 9.7 %slice-start.1 = ((s8[16777216]{0:T(1024)(128)(4,1)}), s8[4194304]{0:T(1024)(128)(4,1)S(1)}, s32[]{:S(2)}) async-start(s8[16777216]{0:T(1024)(128)(4,1)} %bitcast.13), calls=%async_computation.5 | async-start | bytes 8388608
  68.9 9.7 %slice-start.2 = ((s8[16777216]{0:T(1024)(128)(4,1)}), s8[4194304]{0:T(1024)(128)(4,1)S(1)}, s32[]{:S(2)}) async-start(s8[16777216]{0:T(1024)(128)(4,1)} %bitcast.13), calls=%async_computation.6 | async-start | bytes 8388608
  68.9 9.7 %slice-start.3 = ((s8[16777216]{0:T(1024)(128)(4,1)}), s8[4194304]{0:T(1024)(128)(4,1)S(1)}, s32[]{:S(2)}) async-start(s8[16777216]{0:T(1024)(128)(4,1)} %bitcast.13), calls=%async_computation.7 | async-start | bytes 8388608

commit v6 on v5

--- a/solution.py
+++ b/solution.py
@@ -215,25 +215,29 @@
     there = lax.broadcasted_iota(jnp.int32, (rows, rows), 1)
     later = (there > here).astype(F32).astype(BF16)
     copies = []
-    for i, c in enumerate(range(0, width, 256)):
+    for c in range(0, width, 256):
         at = slice(c, c + 256)
         pre = jnp.dot(low, dtw_ref[:, at], preferred_element_type=F32) + dtb_ref[:, at]
         small = jnp.exp(-jnp.abs(pre))
         log1p = jnp.where(small < 1e-3, small - 0.5 * small * small, jnp.log(1.0 + small))
         dt = jnp.maximum(pre, 0.0) + log1p
         dt_ref[:, at] = dt
-        copies.append(pltpu.make_async_copy(dt_ref.at[:, at], dt_hbm.at[:, at], sems.at[i]))
-        copies[-1].start()
+        whole = jnp.sum(dt, axis=0, keepdims=True)
+        for h in range(2):
+            sum_ref[c // LANES + h : c // LANES + h + 1, :] = whole[:, lanes_of(h)]
+    copies.append(pltpu.make_async_copy(dt_ref, dt_hbm, sems.at[0]))
+    copies[-1].start()
+    for c in range(0, width, 256):
+        at = slice(c, c + 256)
+        dt = dt_ref[:, at]
         dx = dt * mixed_ref[:, at].astype(F32)
         rem = jnp.dot(later, dt.astype(BF16), preferred_element_type=F32)
-        whole = jnp.sum(dt, axis=0, keepdims=True)
         ends = jnp.zeros((STATE, 256), F32)
         for n in range(STATE):
             part = (jnp.exp2(rem * rate_ref[n : n + 1, at]) * dx).astype(BF16)
             ends = ends + jnp.dot(enter_ref[STATE * n : STATE * (n + 1), :], part, preferred_element_type=F32)
         for h in range(2):
             j = c // LANES + h
-            sum_ref[j : j + 1, :] = whole[:, lanes_of(h)]
             for k in range(Z):
                 send_ref[PACK * k + STATE * j : PACK * k + STATE * (j + 1), :] = ends[:, lanes_of(h)].astype(BF16)
     for k in range(Z):
@@ -256,7 +260,7 @@
             pltpu.VMEM((rows, width), F32),
             pltpu.VMEM((STATE * STATE, rows), BF16),
             pltpu.VMEM((TILES, LANES), F32),
-            pltpu.SemaphoreType.DMA((width // 256,)),
+            pltpu.SemaphoreType.DMA((1,)),
         ],
         compiler_params=params(12),
         name="state",

time: 81.2 us -> 81.5 us (level)
  no operation moved by 1% of the time
where the time goes in v6:
time: 81.5 us; the launch traced here: 81 us
  blocking collectives  42.4 us (52%)
  Pallas kernels  20.3 us (25%)
  starting transfers between devices  8.77 us (11%)
  waiting for transfers between devices  7.49 us (9%)
  local copies, waits for them, and re-layouts  1.95 us (2%)
    all_to_all x1, blocking collectives, shards(): lax.all_to_all(pair(share, both), 'mp', 0, 0, tiled=True, axis_index_grou...  17 us
    all_to_all x1, blocking collectives, shards(): lax.all_to_all(total(parts), 'mp', 0, 0, tiled=True, axis_index_groups=on_y)  11.8 us
    pallas_call x1, Pallas kernels, local(): pl.pallas_call(local_kernel, out_shape=(flat, pltpu.HBM((rows * STATE * T...  10.2 us
    all_to_all x1, blocking collectives, shards(): got = lax.all_to_all(ends, 'seq', 0, 0, tiled=True, axis_index_groups=on_x)  9.5 us
    ppermute x1, waiting for transfers between devices, shards(): lax.ppermute(inputs[rows - 8:], 'seq', [(s, s + 1) for s in range(seq - 1)])  6.02 us
    pallas_call x1, Pallas kernels, state(): pl.pallas_call(state_kernel, out_shape=(pltpu.HBM((rows, width), F32), pl...  4.77 us
    all_to_all x1, starting transfers between devices, shards(): got = lax.all_to_all(ends, 'seq', 0, 0, tiled=True, axis_index_groups=on_z)  4.51 us
    ppermute x1, starting transfers between devices, shards(): lax.ppermute(inputs[rows - 8:], 'seq', [(s, s + 1) for s in range(seq - 1)])  4.27 us
  transfers between devices with their start and end apart: 2, of which 2 were waited for; matrix products, arithmetic and copies ran while one was open for 0% of the time, Pallas kernels for 15%

profile of v6, /device:TPU:2, one launch (start us, length us, event | category | flops | bytes accessed | tf_op | source)
XLA Modules:
  0.0 81.0 jit_solution(16439669320543705284)
XLA Ops:
  0.0 0.7 slice.3
  0.7 4.3 %collective-permute-start = (bf16[8,1024]{1,0:T(8,128)(2,1)S(1)}, bf16[8,1024]{1,0:T(8,128)(2,1)S(1)}, u32[]{:S(2)}, u32[]{:S(2)}) collective-permute-start(bf16[8,1024]{1,0:T(8,128)(2,1)S(1)} %slice.3), channel_id=1, source_target_pairs={{0,16},{16,32},{32,48},{48,64},{64,80},{80,96},{96,112},{112,128},... | collective-permute-start | bytes 49160 | tf_op jit(solution)/shard_map/ppermute | solution.py:480
  5.0 2.3 %mix.1 = (bf16[256,1024]{1,0:T(8,128)(2,1)S(1)}, f32[8,1024]{1,0:T(8,128)S(1)}, f32[4,1024]{1,0:T(4,128)S(1)}, f32[1,1024]{1,0:T(1,128)S(1)}, bf16[544,1024]{1,0...) custom-call(bf16[256,1024]{1,0:T(8,128)(2,1)} %x_hbm.1, ...), custom_call_target="tpu_custom_call" | custom-call | flops 20000000 | bytes 5000000 | tf_op jit(solution)/shard_map/mix/pallas_call | solution.py:76
  7.3 6.0 %collective-permute-done.halo_ref = bf16[8,1024]{1,0:T(8,128)(2,1)S(1)} collective-permute-done((bf16[8,1024]{1,0:T(8,128)(2,1)S(1)}, bf16[8,1024]{1,0:T(8,128)(2,1)S(1)}, u32[]{:S(2)}, u32[]{:S(2)}) %collective-permute-start) | collective-permute-done | bytes 16416 | tf_op jit(solution)/shard_map/ppermute | solution.py:480
  13.3 0.7 project.1
  14.0 2.0 %all_gather.6.got_ref = bf16[256,544]{1,0:T(8,128)(2,1)S(1)} all-gather(bf16[128,544]{1,0:T(8,128)(2,1)S(1)} %get-tuple-element.31), channel_id=1, replica_groups={{0,1},{2,3},{4,5},{6,7},{8,9},{10,11},{12,13},{14,15},{16,17},{18,19},{..., dimensions={0}, use_global_device_ids=true | all-gather | bytes 417792 | tf_op jit(solution)/shard_map/all_gather | solution.py:492
  16.1 17.0 %all_to_all.45 = bf16[8,16,544]{2,1,0:T(8,128)(2,1)S(1)} all-to-all(bf16[8,16,544]{2,1,0:T(8,128)(2,1)S(1)} %bitcast.17), channel_id=1, replica_groups={{0,2,4,6,8,10,12,14},{1,3,5,7,9,11,13,15},{16,18,20,22,24,26,28,30},{17..., dimensions={0} | all-to-all | bytes 278528 | tf_op jit(solution)/shard_map/all_to_all | solution.py:493
  33.1 11.8 %all_to_all.46 = bf16[8,16,544]{2,1,0:T(8,128)(2,1)S(1)} all-to-all(bf16[8,16,544]{2,1,0:T(8,128)(2,1)S(1)} %bitcast.16), channel_id=1, replica_groups={{0,2,4,6,8,10,12,14},{1,3,5,7,9,11,13,15},{16,18,20,22,24,26,28,30},{17..., dimensions={0} | all-to-all | bytes 278528 | tf_op jit(solution)/shard_map/all_to_all | solution.py:494
  44.9 2.0 %all_gather.7.g_ref = bf16[256,544]{1,0:T(8,128)(2,1)S(1)} all-gather(bf16[128,544]{1,0:T(8,128)(2,1)S(1)} %bitcast.21), channel_id=1, replica_groups={{0,1},{2,3},{4,5},{6,7},{8,9},{10,11},{12,13},{14,15},{16,17},{18,19},{..., dimensions={0}, use_global_device_ids=true | all-gather | bytes 417792 | tf_op jit(solution)/shard_map/all_gather | solution.py:495
  47.0 4.8 %state.1 = (f32[256,1024]{1,0:T(8,128)}, bf16[1152,128]{1,0:T(8,128)(2,1)}) custom-call(bf16[256,544]{1,0:T(8,128)(2,1)S(1)} %all_gather.7.g_ref, bf16[512,1024]{1,0:T(8,128)(2,1)S(1)} %get-tuple-element.32.dtw_ref, f32[1,1024]{1,0:T(1,128)S(1)} %get-tuple-element.33.dtb_ref, bf16[256,1024]{1,0:T(8,128)(2,1)S(1)} %get-tuple-element.34.mixed_ref, ...), custom_call_target="tpu_custom_call" | custom-call | tf_op jit(solution)/shard_map/state/pallas_call | solution.py:251
  51.7 4.5 %all-to-all-start.2 = ((bf16[8,144,128]{2,1,0:T(8,128)(2,1)}), bf16[8,144,128]{2,1,0:T(8,128)(2,1)S(1)}, u32[]{:S(2)}, u32[]{:S(2)}) async-start(bf16[8,144,128]{2,1,0:T(8,128)(2,1)} %bitcast.9), calls=%async_computation.2 | async-start | bytes 589824 | tf_op jit(solution)/shard_map/all_to_all | solution.py:497
  56.2 0.0 copy-start
  56.2 1.2 %copy-done = f32[256,1024]{1,0:T(8,128)S(1)} copy-done((f32[256,1024]{1,0:T(8,128)S(1)}, f32[256,1024]{1,0:T(8,128)}, u32[]{:S(2)}) %copy-start) | copy-done | bytes 1048600
  57.5 10.2 %local.1 = (f32[2048,128]{1,0:T(8,128)S(1)}, f32[32768,128]{1,0:T(8,128)}, f32[16,1024]{1,0:T(8,128)S(1)}) custom-call(bf16[256,544]{1,0:T(8,128)(2,1)S(1)} %all_gather.7.g_ref, f32[256,1024]{1,0:T(8,128)S(1)} %copy-done, f32[16,1024]{1,0:T(8,128)S(1)} %get-tuple-element.35.rate_ref.decay_ref, bf16[256,1024]{1,0:T(8,128)(2,1)S(1)} %get-tuple-element.34.mixed_ref, ...), custom_call_target="tpu_custom_call" | custom-call | flops 60000000 | bytes 15000000 | tf_op jit(solution)/shard_map/local/pallas_call | solution.py:328
  67.6 1.5 %all-to-all-done.2 = bf16[8,144,128]{2,1,0:T(8,128)(2,1)S(1)} async-done(((bf16[8,144,128]{2,1,0:T(8,128)(2,1)}), bf16[8,144,128]{2,1,0:T(8,128)(2,1)S(1)}, u32[]{:S(2)}, u32[]{:S(2)}) %all-to-all-start.2) | async-done | bytes 294944 | tf_op jit(solution)/shard_map/all_to_all | solution.py:497
  69.1 0.0 slice-start
  69.1 0.0 slice-start.1
  69.1 0.0 slice-start.2
  69.1 0.0 slice-start.3
  69.1 0.1 merge.1
  69.3 9.5 %all_to_all.47 = bf16[4,144,128]{2,1,0:T(8,128)(2,1)S(1)} all-to-all(bf16[4,144,128]{2,1,0:T(8,128)(2,1)S(1)} %bitcast.20), channel_id=1, replica_groups={{0,128,256,384},{16,144,272,400},{32,160,288,416},{48,176,304,432},{64,..., dimensions={0} | all-to-all | bytes 294912 | tf_op jit(solution)/shard_map/all_to_all | solution.py:500
  78.8 0.0 slice-done
  78.8 0.0 slice-done.1
  78.8 0.0 slice-done.2
  78.8 0.0 slice-done.3
  78.8 2.2 %finish.1 = bf16[256,1024]{1,0:T(8,128)(2,1)} custom-call(bf16[576,128]{1,0:T(8,128)(2,1)S(1)} %bitcast.18, f32[128,128]{1,0:T(8,128)S(1)} %get-tuple-element.41.state_ref, f32[8,128]{1,0:T(8,128)S(1)} %get-tuple-element.42.before_ref, f32[16,1024]{1,0:T(8,128)S(1)} %get-tuple-element.39.rate_ref, f32[2048,128]{1,0:T(8,128)S(1)} %get-tuple-element.43.y_ref, ...), custom_call_target="tpu_custom_call" | custom-call | tf_op jit(solution)/shard_map/finish/pallas_call | solution.py:454
  (3 shorter events, 0.1 us)
Async XLA Ops:
  0.7 12.6 %collective-permute-start = (bf16[8,1024]{1,0:T(8,128)(2,1)S(1)}, bf16[8,1024]{1,0:T(8,128)(2,1)S(1)}, u32[]{:S(2)}, u32[]{:S(2)}) collective-permute-start(bf16[8,1024]{1,0:T(8,128)(2,1)S(1)} %slice.3), channel_id=1, source_target_pairs={{0,16},{16,32},{32,48},{48,64},{64,80},{80,96},{96,112},{112,128},... | collective-permute-start | bytes 49160 | tf_op jit(solution)/shard_map/ppermute | solution.py:480
  51.7 17.4 %all-to-all-start.2 = ((bf16[8,144,128]{2,1,0:T(8,128)(2,1)}), bf16[8,144,128]{2,1,0:T(8,128)(2,1)S(1)}, u32[]{:S(2)}, u32[]{:S(2)}) async-start(bf16[8,144,128]{2,1,0:T(8,128)(2,1)} %bitcast.9), calls=%async_computation.2 | async-start | bytes 589824 | tf_op jit(solution)/shard_map/all_to_all | solution.py:497
  56.2 1.2 %copy-start = (f32[256,1024]{1,0:T(8,128)S(1)}, f32[256,1024]{1,0:T(8,128)}, u32[]{:S(2)}) copy-start(f32[256,1024]{1,0:T(8,128)} %get-tuple-element.37.step_ref) | copy-start | bytes 3145732
  69.1 9.7 %slice-start = ((s8[16777216]{0:T(1024)(128)(4,1)}), s8[4194304]{0:T(1024)(128)(4,1)S(1)}, s32[]{:S(2)}) async-start(s8[16777216]{0:T(1024)(128)(4,1)} %bitcast.13), calls=%async_computation.4 | async-start | bytes 8388608
  69.1 9.7 %slice-start.1 = ((s8[16777216]{0:T(1024)(128)(4,1)}), s8[4194304]{0:T(1024)(128)(4,1)S(1)}, s32[]{:S(2)}) async-start(s8[16777216]{0:T(1024)(128)(4,1)} %bitcast.13), calls=%async_computation.5 | async-start | bytes 8388608
  69.1 9.7 %slice-start.2 = ((s8[16777216]{0:T(1024)(128)(4,1)}), s8[4194304]{0:T(1024)(128)(4,1)S(1)}, s32[]{:S(2)}) async-start(s8[16777216]{0:T(1024)(128)(4,1)} %bitcast.13), calls=%async_computation.6 | async-start | bytes 8388608
  69.1 9.7 %slice-start.3 = ((s8[16777216]{0:T(1024)(128)(4,1)}), s8[4194304]{0:T(1024)(128)(4,1)S(1)}, s32[]{:S(2)}) async-start(s8[16777216]{0:T(1024)(128)(4,1)} %bitcast.13), calls=%async_computation.7 | async-start | bytes 8388608
